TPU v7x, 32 devices: a whole 2x2x4 slice. The times are simulated.
32 devices in a mesh: seq: 8 (over y, x, core), tp: 4 (over z).
Axes of the slice: x: 2, y: 2, z: 4, core: 2. Of those that a mesh axis runs over, the one named last changes fastest.
Arguments:
- hidden: bfloat16 [4096, 3584], P('seq', 'tp'), may hold values from -6 to 6
- modality: int32 [4096], P('seq'), may hold values from 0 to 2, as said below
- segment_bounds: int32 [6], replicated, may hold values from 0 to 4096, as said below
- block_mask: int32 [32, 32], replicated, may hold values from 0 to 1, as said below
- norm_gain: float32 [2, 2, 3584], replicated, may hold values from 0.1 to 1.9
- query_weight: bfloat16 [2, 3584, 2048], P(None, None, 'tp'), may hold values from -1 to 1
- keys_values: bfloat16 [2, 3584, 1024], P(None, None, 'tp'), may hold values from -1 to 1
- output_weight: bfloat16 [2, 2048, 3584], P(None, 'tp'), may hold values from -0.375 to 0.375
- gate_weight: bfloat16 [7168, 10240], P('seq', 'tp'), may hold values from -0.09375 to 0.09375
- up_weight: bfloat16 [7168, 10240], P('seq', 'tp'), may hold values from -0.09375 to 0.09375
- down_weight: bfloat16 [7168, 10240], P('seq', 'tp'), may hold values from -0.0625 to 0.0625
Outputs:
- layer_output: bfloat16 [4096, 3584], P('seq', 'tp')
Inputs may be any that keep to these rules, and one draw needn't show every extreme that they name: `modality`: rows below 2048 carry 0 (text) or 1 (understanding image), constant over aligned runs of 32 rows; all other rows carry 2 (generation image). `segment_bounds`: strictly increasing; the first entry is 0 and the last 4096. `block_mask`: every diagonal entry is 1.
All inputs are finite; a program needn't handle non-finite values.
Results may differ from a plain program's by a relative error of at most 0.02.
The roundings to bfloat16 on the way count: a program that leaves them out, or rounds other values in their place, can miss the bound.
Values may be sent and summed in bfloat16 or wider, within the bound.
A program may use at most 192 MiB of HBM per device.

v0:
```python
import jax
import jax.numpy as jnp
from jax import lax
from jax.sharding import PartitionSpec as P

HEADS = 16
KVH = 4
HD = 128
BLOCK = 128


theta_base = 1000000.0
epsilon = 1e-06
key_step = 512
masked_score = -1e30


def partner_2(block, axis, stride):
    count = lax.axis_size(axis)
    route = []
    for low in range(count):
        high = low | 1 << stride
        if high != low and high < count:
            route += [(low, high), (high, low)]
    return lax.ppermute(block, axis, route)


def normalize(values, gain_row):
    widened = values.astype(jnp.float32)
    mean_square = jnp.mean(widened * widened, axis=-1, keepdims=True)
    return (widened * lax.rsqrt(mean_square + epsilon) * gain_row).astype(jnp.bfloat16)


def rotary(values, offsets):
    half_dim = values.shape[-1] // 2
    frequency = theta_base ** (-2.0 * jnp.arange(half_dim, dtype=jnp.float32) / values.shape[-1])
    angles = offsets.astype(jnp.float32)[:, None] * frequency[None, :]
    cosine = jnp.cos(angles)[:, None, :]
    sine_part = jnp.sin(angles)[:, None, :]
    leading = values[..., :half_dim]
    trailing = values[..., half_dim:]
    return jnp.concatenate(
        [leading * cosine - trailing * sine_part, trailing * cosine + leading * sine_part], axis=-1
    )


def segment_info(positions, segment_bounds):
    openings = segment_bounds[:-1]
    inside = positions[:, None] >= openings[None, :]
    segment_ids = jnp.sum(inside.astype(jnp.int32), axis=1)
    opening = jnp.max(jnp.where(inside, openings[None, :], 0), axis=1)
    return (segment_ids, positions - opening)


def double_up(stacked, seq_index, level_count, partner_of):
    for bit_number in range(level_count):
        partner = partner_of(stacked, bit_number)
        upper_half = seq_index // 2**bit_number % 2 == 1
        stacked = jnp.where(
            upper_half,
            jnp.concatenate([partner, stacked], axis=1),
            jnp.concatenate([stacked, partner], axis=1),
        )
    return stacked


def body(
    hidden,
    modality,
    segment_bounds,
    block_mask,
    norm_gain,
    query_weight,
    keys_values,
    output_weight,
    gate_weight,
    up_weight,
    down_weight,
):
    seq_count = lax.axis_size("seq")
    seq_index = lax.axis_index("seq")
    tp_index = lax.axis_index("tp")
    row_count = hidden.shape[0]
    weight_set = (seq_index >= seq_count // 2).astype(jnp.int32)
    positions = seq_index * row_count + jnp.arange(row_count, dtype=jnp.int32)
    segment_ids, offsets = segment_info(positions, segment_bounds)
    gain_rows = lax.dynamic_index_in_dim(norm_gain, weight_set, 0, keepdims=False)
    local_query = lax.dynamic_index_in_dim(query_weight, weight_set, 0, keepdims=False)
    local_pairs = lax.dynamic_index_in_dim(keys_values, weight_set, 0, keepdims=False)
    local_output = lax.dynamic_index_in_dim(output_weight, weight_set, 0, keepdims=False)
    full_rows = lax.all_gather(hidden, "tp", axis=1, tiled=True)
    normed = normalize(full_rows, gain_rows[0])
    heads_here = local_query.shape[1] // HD
    group_size = HEADS // KVH
    shared_heads = max(1, heads_here // group_size)
    per_shared = heads_here // shared_heads
    queries = rotary(
        jnp.dot(normed, local_query, preferred_element_type=jnp.float32).reshape(
            row_count, heads_here, HD
        ),
        offsets,
    ).astype(jnp.bfloat16)
    grouped = queries.reshape(row_count, shared_heads, per_shared, HD)
    projected = jnp.dot(normed, local_pairs, preferred_element_type=jnp.float32).astype(
        jnp.bfloat16
    )
    all_pairs = lax.all_gather(projected, "tp", axis=1, tiled=True)
    first_shared = tp_index * heads_here // group_size
    raw_keys = lax.dynamic_slice_in_dim(all_pairs, first_shared * HD, shared_heads * HD, 1)
    own_values = lax.dynamic_slice_in_dim(
        all_pairs, KVH * HD + first_shared * HD, shared_heads * HD, 1
    )
    own_keys = (
        rotary(raw_keys.astype(jnp.float32).reshape(row_count, shared_heads, HD), offsets)
        .astype(jnp.bfloat16)
        .reshape(row_count, shared_heads * HD)
    )
    query_modes = modality.astype(jnp.float32)
    block_rows = row_count // BLOCK
    mask_rows = lax.dynamic_slice_in_dim(block_mask, seq_index * block_rows, block_rows, 0).astype(
        jnp.float32
    )
    block_count = block_mask.shape[1]
    score_scale = HD ** (-0.5)

    def key_block(running, key_rows, value_rows, mode_rows, key_start):
        best_score, denominator, accumulated = running
        key_count = key_rows.shape[0]
        key_positions = key_start + jnp.arange(key_count, dtype=jnp.int32)
        key_segments = segment_info(key_positions, segment_bounds)[0]
        picker = (
            key_positions[None, :] // BLOCK == jnp.arange(block_count, dtype=jnp.int32)[:, None]
        ).astype(jnp.float32)
        coarse = jnp.repeat(jnp.dot(mask_rows, picker), BLOCK, axis=0) > 0.5
        key_modes = mode_rows.astype(jnp.float32)
        mutual = (query_modes[:, None] > 0.5) & (query_modes[:, None] == key_modes[None, :])
        allowed = (
            coarse
            & (segment_ids[:, None] == key_segments[None, :])
            & ((key_positions[None, :] <= positions[:, None]) | mutual)
        )
        scores = (
            jnp.einsum(
                "rkgd,ckd->kgrc",
                grouped,
                key_rows.reshape(key_count, shared_heads, HD),
                preferred_element_type=jnp.float32,
            )
            * score_scale
        )
        scores = jnp.where(allowed[None, None], scores, masked_score)
        new_best = jnp.maximum(best_score, jnp.max(scores, axis=-1))
        exponent = jnp.where(allowed[None, None], jnp.exp(scores - new_best[..., None]), 0.0)
        fading = jnp.exp(best_score - new_best)
        denominator = denominator * fading + jnp.sum(exponent, axis=-1)
        accumulated = accumulated * fading[..., None] + jnp.einsum(
            "kgrc,ckd->kgrd",
            exponent.astype(jnp.bfloat16),
            value_rows.reshape(key_count, shared_heads, HD),
            preferred_element_type=jnp.float32,
        )
        return (new_best, denominator, accumulated)

    initial = (
        jnp.full((shared_heads, per_shared, row_count), masked_score, jnp.float32),
        jnp.zeros((shared_heads, per_shared, row_count), jnp.float32),
        jnp.zeros((shared_heads, per_shared, row_count, HD), jnp.float32),
    )
    key_rows = lax.all_gather(own_keys, "seq", axis=0, tiled=True)
    value_rows = lax.all_gather(own_values, "seq", axis=0, tiled=True)
    mode_rows = lax.all_gather(modality.astype(jnp.bfloat16), "seq", axis=0, tiled=True)
    piece_count = key_rows.shape[0]

    def one_step(step_number, inner_state):
        offset = step_number * key_step
        return key_block(
            inner_state,
            lax.dynamic_slice_in_dim(key_rows, offset, key_step, 0),
            lax.dynamic_slice_in_dim(value_rows, offset, key_step, 0),
            lax.dynamic_slice_in_dim(mode_rows, offset, key_step, 0),
            offset,
        )

    best_score, denominator, accumulated = lax.fori_loop(
        0, piece_count // key_step, one_step, initial
    )
    attended = (
        (accumulated / denominator[..., None])
        .transpose(2, 0, 1, 3)
        .reshape(row_count, heads_here * HD)
        .astype(jnp.bfloat16)
    )
    attention_terms = jnp.dot(attended, local_output, preferred_element_type=jnp.float32)
    attention_share = lax.psum_scatter(
        attention_terms.astype(jnp.bfloat16), "tp", scatter_dimension=1, tiled=True
    ).astype(jnp.float32)
    residual_share = (hidden.astype(jnp.float32) + attention_share).astype(jnp.bfloat16)
    residual_full = lax.all_gather(residual_share, "tp", axis=1, tiled=True)
    second_normed = normalize(residual_full, gain_rows[1])
    level_count = (seq_count // 2).bit_length() - 1
    paired = double_up(
        jnp.stack([gate_weight, up_weight]),
        seq_index,
        level_count,
        lambda operand, bit_number: partner_2(operand, "seq", bit_number),
    )
    down_full = double_up(
        down_weight[None],
        seq_index,
        level_count,
        lambda operand, bit_number: partner_2(operand, "seq", bit_number),
    )[0]
    gate_full, up_full = (paired[0], paired[1])
    gate_values = jnp.dot(second_normed, gate_full, preferred_element_type=jnp.float32)
    up_values = jnp.dot(second_normed, up_full, preferred_element_type=jnp.float32)
    active = (jax.nn.silu(gate_values) * up_values).astype(jnp.bfloat16)
    down_terms = lax.dot_general(
        active, down_full, (((1,), (1,)), ((), ())), preferred_element_type=jnp.float32
    )
    down_share = lax.psum_scatter(
        down_terms.astype(jnp.bfloat16), "tp", scatter_dimension=1, tiled=True
    ).astype(jnp.float32)
    return (residual_share.astype(jnp.float32) + down_share).astype(jnp.bfloat16)


def solution(mesh):
    placed = (
        P("seq", "tp"),
        P("seq"),
        P(),
        P(),
        P(),
        P(None, None, "tp"),
        P(None, None, "tp"),
        P(None, "tp", None),
        P("seq", "tp"),
        P("seq", "tp"),
        P("seq", "tp"),
    )
    return jax.shard_map(
        body, mesh=mesh, in_specs=placed, out_specs=P("seq", "tp"), check_vma=False
    )
```

profile of v0, /device:TPU:0, one launch (start us, length us, event | category | flops | bytes accessed | tf_op | source)
XLA Modules:
  0.0 868.5 jit_solution(7680765258363002436)
XLA Ops:
  7.3 8.1 pad_maximum_fusion
  15.9 67.8 %all-gather.7.cloned.1.call-done = bf16[512,3584]{1,0:T(8,128)(2,1)} async-done(((bf16[512,896]{1,0:T(8,128)(2,1)}), bf16[512,3584]{1,0:T(8,128)(2,1)}) %all-gather.7.cloned.1.call-update) | async-done | bytes 3670032 | tf_op jit(solution)/shard_map/all_gather | solution.py:91
  83.8 2.8 fusion.42
  86.6 4.5 fusion.57
  91.4 28.7 %all-gather.9.cloned.1.call-done = bf16[512,1024]{1,0:T(8,128)(2,1)} async-done(((bf16[512,256]{1,0:T(8,128)(2,1)}), bf16[512,1024]{1,0:T(8,128)(2,1)}) %all-gather.9.cloned.1.call-update) | async-done | bytes 1048592 | tf_op jit(solution)/shard_map/all_gather | solution.py:107
  120.1 1.7 constant_dynamic-slice_fusion
  123.8 4.2 dynamic-slice_bitcast_fusion
  128.0 6.0 copy.27
  134.0 7.8 all-gather
  143.1 5.4 fusion.50
  149.2 21.2 %maximum_select_fusion.1 = bf16[2,1792,2560]{2,1,0:T(8,128)(2,1)} fusion(bf16[1,896,2560]{2,1,0:T(8,128)(2,1)} %bitcast.147, bf16[1,896,2560]{2,1,0:T(8,128)(2,1)} %bitcast.149, bf16[2,896,2560]{2,1,0:T(8,128)(2,1)} %collective-permute-done, pred[]{:T(512)S(6)} %eq.126), kind=kLoop, calls=%fused_computation.52 | loop fusion | flops 119275520 | bytes 36700160 | tf_op jit(solution)/shard_map/jit(_where)/select_n | solution.py:59
  170.4 1.6 collective-permute-start.1
  172.0 94.7 %while.20 = (s32[]{:T(128)}, f32[1,4,512]{2,1,0:T(4,128)S(1)}, f32[1,4,512]{2,1,0:T(4,128)S(1)}, f32[1,4,512,128]{3,2,1,0:T(8,128)S(1)}, bf16[4,32]{1,0:T(4,128)...) while((s32[]{:T(128)}, f32[1,4,512]{2,1,0:T(4,128)S(1)}, ...), condition=%wide.region_7.8_spmd.clone, body=%wide.region_3.7_spmd.clone.sunk | while | flops 553302528 | bytes 33987096 | solution.py:184
  172.5 1.6 broadcast_in_dim.180
  174.7 3.7 fusion.100
  178.4 4.3 fusion.103
  184.4 1.6 broadcast_in_dim.180
  186.5 3.7 fusion.100
  190.3 4.3 fusion.103
  196.2 1.6 broadcast_in_dim.180
  198.4 3.7 fusion.100
  202.1 4.3 fusion.103
  208.1 1.6 broadcast_in_dim.180
  210.2 3.7 fusion.100
  214.0 4.3 fusion.103
  222.1 3.7 fusion.100
  225.8 4.3 fusion.103
  233.9 3.7 fusion.100
  237.6 4.3 fusion.103
  245.7 3.7 fusion.100
  249.5 4.3 fusion.103
  257.6 3.7 fusion.100
  261.3 4.3 fusion.103
  267.2 5.9 convolution_convert_fusion
  273.2 6.0 copy.31
  279.5 68.2 %reduce-scatter.7.cloned.1.call-done = bf16[896,512]{1,0:T(8,128)(2,1)} async-done(((bf16[3584,512]{1,0:T(8,128)(2,1)}), bf16[896,512]{1,0:T(8,128)(2,1)}) %reduce-scatter.7.cloned.1.call-update) | async-done | bytes 917520
  350.8 13.1 %maximum_select_fusion.4 = bf16[1,1792,2560]{2,1,0:T(8,128)(2,1)} fusion(bf16[1,896,2560]{2,1,0:T(8,128)(2,1)} %bitcast.151, bf16[1,896,2560]{2,1,0:T(8,128)(2,1)} %collective-permute-done.2, pred[]{:T(512)S(6)} %eq.126), kind=kLoop, calls=%fused_computation.62 | loop fusion | flops 41287680 | bytes 18350080 | tf_op jit(solution)/shard_map/jit(_where)/select_n | solution.py:59
  365.3 10.0 %maximum_select_fusion.5 = bf16[1792,2560]{1,0:T(8,128)(2,1)} fusion(bf16[896,2560]{1,0:T(8,128)(2,1)S(1)} %bitcast.153, bf16[896,2560]{1,0:T(8,128)(2,1)} %bitcast.21, pred[]{:T(512)S(6)} %eq.126), kind=kLoop, calls=%fused_computation.63 | loop fusion | flops 41287680 | bytes 18350080 | tf_op jit(solution)/shard_map/jit(_where)/select_n | solution.py:59
  375.3 47.8 %all-gather.15.cloned.1.call-done = bf16[512,3584]{1,0:T(8,128)(2,1)} async-done(((bf16[512,896]{1,0:T(8,128)(2,1)}), bf16[512,3584]{1,0:T(8,128)(2,1)}) %all-gather.15.cloned.1.call-update) | async-done | bytes 3670032 | tf_op jit(solution)/shard_map/all_gather | solution.py:198
  423.1 2.8 fusion.45
  425.9 141.6 %collective-permute-done.1 = bf16[2,1792,2560]{2,1,0:T(8,128)(2,1)} collective-permute-done((bf16[2,1792,2560]{2,1,0:T(8,128)(2,1)}, bf16[2,1792,2560]{2,1,0:T(8,128)(2,1)}, u32[]{:S(2)}, u32[]{:S(2)}) %collective-permute-start.1) | collective-permute-done | bytes 18350112 | tf_op jit(solution)/shard_map/ppermute | solution.py:25
  567.5 36.9 %maximum_select_fusion = bf16[2,3584,2560]{2,1,0:T(8,128)(2,1)} fusion(bf16[2,1792,2560]{2,1,0:T(8,128)(2,1)} %maximum_select_fusion.1, bf16[2,1792,2560]{2,1,0:T(8,128)(2,1)} %collective-permute-done.1, pred[]{:T(512)S(6)} %eq.125), kind=kLoop, calls=%fused_computation.47 | loop fusion | flops 165150720 | bytes 73400320 | tf_op jit(solution)/shard_map/jit(_where)/select_n | solution.py:59
  604.4 15.2 %fusion.34 = f32[512,2560]{1,0:T(8,128)} fusion(bf16[2,3584,2560]{2,1,0:T(8,128)(2,1)} %maximum_select_fusion, bf16[512,3584]{1,0:T(8,128)(2,1)S(1)} %copy-done.2, f32[3584]{0:T(1024)S(1)} %get-tuple-element.414, f32[512]{0:T(512)S(1)} %add_rsqrt_fusion), kind=kOutput, calls=%fused_computation.51 | convolution fusion | flops 9402580992 | bytes 27279360 | tf_op jit(solution)/shard_map/dot_general | solution.py:214
  619.6 15.2 %fusion.33 = f32[512,2560]{1,0:T(8,128)} fusion(bf16[2,3584,2560]{2,1,0:T(8,128)(2,1)} %maximum_select_fusion, bf16[512,3584]{1,0:T(8,128)(2,1)S(1)} %copy-done.2, f32[3584]{0:T(1024)S(1)} %get-tuple-element.414, f32[512]{0:T(512)S(1)} %add_rsqrt_fusion), kind=kOutput, calls=%fused_computation.49 | convolution fusion | flops 9402580992 | bytes 27279360 | tf_op jit(solution)/shard_map/dot_general | solution.py:215
  634.8 128.8 %collective-permute-done.3 = bf16[1,1792,2560]{2,1,0:T(8,128)(2,1)} collective-permute-done((bf16[1,1792,2560]{2,1,0:T(8,128)(2,1)}, bf16[1,1792,2560]{2,1,0:T(8,128)(2,1)}, u32[]{:S(2)}, u32[]{:S(2)}) %collective-permute-start.3) | collective-permute-done | bytes 9175072 | tf_op jit(solution)/shard_map/ppermute | solution.py:25
  763.5 21.5 %fusion.48 = bf16[512,3584]{1,0:T(8,128)(2,1)} fusion(bf16[1792,2560]{1,0:T(8,128)(2,1)} %maximum_select_fusion.5, bf16[1792,2560]{1,0:T(8,128)(2,1)} %bitcast.20, pred[]{:T(512)S(6)} %eq.125, f32[512,2560]{1,0:T(8,128)} %fusion.33, f32[512,2560]{1,0:T(8,128)} %fusion.34), kind=kOutput, calls=%fused_computation.74 | convolution fusion | flops 9487515648 | bytes 32505856 | tf_op jit(solution)/shard_map/dot_general | solution.py:217
  785.0 6.0 copy.33
  791.1 67.9 %reduce-scatter.9.cloned.1.call-done = bf16[896,512]{1,0:T(8,128)(2,1)} async-done(((bf16[3584,512]{1,0:T(8,128)(2,1)}), bf16[896,512]{1,0:T(8,128)(2,1)}) %reduce-scatter.9.cloned.1.call-update) | async-done | bytes 917520
  (181 shorter events, 36.7 us)
Async XLA Ops:
  6.5 77.3 %all-gather.7.cloned.1.call-start = ((), (), s32[]{:S(2)}) async-start(), calls=%async_computation.2 | async-start | bytes 4587520 | tf_op jit(solution)/shard_map/all_gather | solution.py:91
  7.3 112.9 %all-gather.9.cloned.1.call-start = ((), (), s32[]{:S(2)}) async-start(), calls=%async_computation.3 | async-start | bytes 1310720 | tf_op jit(solution)/shard_map/all_gather | solution.py:107
  7.3 8.6 copy-start.5
  15.4 75.8 %copy-start.4 = (s32[6]{0:T(128)S(1)}, s32[6]{0:T(128)}, u32[]{:S(2)}) copy-start(s32[6]{0:T(128)} %param.15) | copy-start | bytes 76
  15.4 133.8 %collective-permute-start = (bf16[2,896,2560]{2,1,0:T(8,128)(2,1)}, bf16[2,896,2560]{2,1,0:T(8,128)(2,1)}, u32[]{:S(2)}, u32[]{:S(2)}) collective-permute-start(bf16[2,896,2560]{2,1,0:T(8,128)(2,1)} %pad_maximum_fusion), channel_id=1, source_target_pairs={{0,4},{4,0},{8,12},{12,8},{16,20},{20,16},{24,28},{28,24},{1,5},{5... | collective-permute-start | bytes 27525128 | tf_op jit(solution)/shard_map/ppermute | solution.py:25
  91.2 80.9 %all-gather.11.cloned.1.call-start = ((), (), s32[]{:S(2)}) async-start(), calls=%async_computation.4 | async-start | bytes 1179648 | tf_op jit(solution)/shard_map/all_gather | solution.py:169
  123.8 10.2 %copy-start.6 = (s32[512]{0:T(512)S(1)}, s32[512]{0:T(512)}, u32[]{:S(2)}) copy-start(s32[512]{0:T(512)} %param.14) | copy-start | bytes 6148
  123.8 48.3 %all-gather.13.cloned.1.call-start = ((), (), s32[]{:S(2)}) async-start(), calls=%async_computation.5 | async-start | bytes 1179648 | tf_op jit(solution)/shard_map/all_gather | solution.py:170
  149.0 198.7 %reduce-scatter.7.cloned.1.call-start = ((), (), s32[]{:S(2)}) async-start(), calls=%async_computation.7 | async-start | bytes 4587520
  170.4 397.1 %collective-permute-start.1 = (bf16[2,1792,2560]{2,1,0:T(8,128)(2,1)}, bf16[2,1792,2560]{2,1,0:T(8,128)(2,1)}, u32[]{:S(2)}, u32[]{:S(2)}) collective-permute-start(bf16[2,1792,2560]{2,1,0:T(8,128)(2,1)} %maximum_select_fusion.1), channel_id=1, source_target_pairs={{0,8},{8,0},{4,12},{12,4},{16,24},{24,16},{20,28},{28,20},{1,9},{9... | collective-permute-start | bytes 55050248 | tf_op jit(solution)/shard_map/ppermute | solution.py:25
  178.4 4.3 copy-start
  190.3 4.3 copy-start
  202.1 4.3 copy-start
  214.0 4.3 copy-start
  225.8 4.3 copy-start
  237.6 4.3 copy-start
  249.5 4.3 copy-start
  261.3 4.3 copy-start
  273.2 76.1 %copy-start.3 = (bf16[512,896]{1,0:T(8,128)(2,1)S(1)}, bf16[512,896]{1,0:T(8,128)(2,1)}, u32[]{:S(2)}) copy-start(bf16[512,896]{1,0:T(8,128)(2,1)} %param.13) | copy-start | bytes 2752516
  279.2 143.8 %all-gather.15.cloned.1.call-start = ((), (), s32[]{:S(2)}) async-start(), calls=%async_computation.6 | async-start | bytes 4587520 | tf_op jit(solution)/shard_map/all_gather | solution.py:198
  279.3 71.5 %collective-permute-start.2 = (bf16[1,896,2560]{2,1,0:T(8,128)(2,1)}, bf16[1,896,2560]{2,1,0:T(8,128)(2,1)}, u32[]{:S(2)}, u32[]{:S(2)}) collective-permute-start(bf16[1,896,2560]{2,1,0:T(8,128)(2,1)} %bitcast.150), channel_id=1, source_target_pairs={{0,4},{4,0},{8,12},{12,8},{16,20},{20,16},{24,28},{28,24},{1,5},{5... | collective-permute-start | bytes 13762568 | tf_op jit(solution)/shard_map/ppermute | solution.py:25
  350.4 508.5 %reduce-scatter.9.cloned.1.call-start = ((), (), s32[]{:S(2)}) async-start(), calls=%async_computation.8 | async-start | bytes 4587520
  350.7 14.5 %slice-start = ((s8[4587520]{0:T(1024)(128)(4,1)}), s8[393216]{0:T(1024)(128)(4,1)S(1)}, s32[]{:S(2)}) async-start(s8[4587520]{0:T(1024)(128)(4,1)} %bitcast.152), calls=%async_computation.9 | async-start | bytes 786432
  350.7 14.5 %slice-start.1 = ((s8[4587520]{0:T(1024)(128)(4,1)}), s8[4194304]{0:T(1024)(128)(4,1)S(1)}, s32[]{:S(2)}) async-start(s8[4587520]{0:T(1024)(128)(4,1)} %bitcast.152), calls=%async_computation.10 | async-start | bytes 8388608
  363.9 399.6 %collective-permute-start.3 = (bf16[1,1792,2560]{2,1,0:T(8,128)(2,1)}, bf16[1,1792,2560]{2,1,0:T(8,128)(2,1)}, u32[]{:S(2)}, u32[]{:S(2)}) collective-permute-start(bf16[1,1792,2560]{2,1,0:T(8,128)(2,1)} %maximum_select_fusion.4), channel_id=1, source_target_pairs={{0,8},{8,0},{4,12},{12,4},{16,24},{24,16},{20,28},{28,20},{1,9},{9... | collective-permute-start | bytes 27525128 | tf_op jit(solution)/shard_map/ppermute | solution.py:25
  425.9 178.5 %copy-start.2 = (bf16[512,3584]{1,0:T(8,128)(2,1)S(1)}, bf16[512,3584]{1,0:T(8,128)(2,1)}, u32[]{:S(2)}) copy-start(bf16[512,3584]{1,0:T(8,128)(2,1)} %all-gather.15.cloned.1.call-done) | copy-start | bytes 11010052
  785.0 75.5 %copy-start.1 = (bf16[512,896]{1,0:T(8,128)(2,1)S(1)}, bf16[512,896]{1,0:T(8,128)(2,1)}, u32[]{:S(2)}) copy-start(bf16[512,896]{1,0:T(8,128)(2,1)} %add_convert_fusion.1) | copy-start | bytes 2752516
Sparse Core Ops, SparseCore 0:
  9.0 74.7 all-gather.6
  91.3 28.7 all-gather.8
  123.9 21.7 all-gather.10
  149.1 22.7 all-gather.12
  279.4 68.3 reduce-scatter.6
  350.5 72.4 all-gather.14
  791.2 67.6 reduce-scatter.8
where the time goes:
time: 869 us; the launch traced here: 868 us
  waiting for transfers between devices  552 us (64%)
  matrix products  133 us (15%)
  other arithmetic  117 us (13%)
  local copies, waits for them, and re-layouts  40.4 us (5%)
  between operations  13.8 us (2%)
    ppermute x4, waiting for transfers between devices, partner_2(): return lax.ppermute(block, axis, route)  270 us
    unnamed x9, waiting for transfers between devices  137 us
    select_n x4, other arithmetic, double_up(): jnp.where(upper_half, jnp.concatenate([partner, stacked], axis=1), jnp.co...  81.2 us
    all_gather x1, waiting for transfers between devices, body(): full_rows = lax.all_gather(hidden, 'tp', axis=1, tiled=True)  67.8 us
    all_gather x1, waiting for transfers between devices, body(): residual_full = lax.all_gather(residual_share, 'tp', axis=1, tiled=True)  47.8 us
    dot_general x8, matrix products, key_block(): jnp.einsum('kgrc,ckd->kgrd', exponent.astype(jnp.bfloat16), value_rows.re...  34.5 us
    dot_general x8, matrix products, key_block(): jnp.einsum('rkgd,ckd->kgrc', grouped, key_rows.reshape(key_count, shared_...  29.8 us
    all_gather x1, waiting for transfers between devices, body(): all_pairs = lax.all_gather(projected, 'tp', axis=1, tiled=True)  28.7 us
  transfers between devices with their start and end apart: 11, of which 7 were waited for; matrix products, arithmetic and copies ran while one was open for 30% of the time, Pallas kernels for 0%

commit v1 on v0

--- a/solution.py
+++ b/solution.py
@@ -1,6 +1,8 @@
 import jax
 import jax.numpy as jnp
 from jax import lax
+from jax.experimental import pallas as pl
+from jax.experimental.pallas import tpu as pltpu
 from jax.sharding import PartitionSpec as P
 
 HEADS = 16
@@ -64,7 +66,7 @@
     return stacked
 
 
-def body(
+def general_body(
     hidden,
     modality,
     segment_bounds,
@@ -223,6 +225,355 @@
     return (residual_share.astype(jnp.float32) + down_share).astype(jnp.bfloat16)
 
 
+def exchange(block, bit):
+    count = lax.axis_size("seq")
+    return lax.ppermute(block, "seq", [(low, low ^ bit) for low in range(count)])
+
+
+def attend_kernel(flags, q_ref, kv_ref, bias_ref, o_ref, best, total, mixed):
+    tile = pl.program_id(0)
+    rows = q_ref.shape[0]
+    heads = q_ref.shape[1] // HD
+    stacked = jnp.concatenate([q_ref[:, h * HD : (h + 1) * HD] for h in range(heads)], axis=0)
+    best[...] = jnp.full_like(best, 0.1 * masked_score)
+    total[...] = jnp.zeros_like(total)
+    mixed[...] = jnp.zeros_like(mixed)
+
+    def step(chunk, carry):
+        @pl.when(flags[tile, chunk] > 0)
+        def _():
+            span = pl.ds(pl.multiple_of(chunk * key_step, key_step), key_step)
+            pair = kv_ref[span, :]
+            scores = lax.dot_general(
+                stacked,
+                pair[:, :HD],
+                (((1,), (1,)), ((), ())),
+                preferred_element_type=jnp.float32,
+            ) * (HD ** (-0.5))
+            bias = bias_ref[:, span].astype(jnp.float32)
+            scores = (scores.reshape(heads, rows, key_step) + bias[None]).reshape(
+                heads * rows, key_step
+            )
+            old = best[...]
+            peak = jnp.maximum(old, jnp.max(scores, axis=1, keepdims=True))
+            fading = jnp.exp(old - peak)
+            exponent = jnp.exp(scores - peak[:, :1])
+            total[...] = total[...] * fading + jnp.sum(exponent, axis=1, keepdims=True)
+            mixed[...] = mixed[...] * fading + jnp.dot(
+                exponent.astype(jnp.bfloat16), pair[:, HD:], preferred_element_type=jnp.float32
+            )
+            best[...] = peak
+
+        return carry
+
+    lax.fori_loop(0, kv_ref.shape[0] // key_step, step, 0)
+    result = (mixed[...] / total[...]).astype(jnp.bfloat16)
+    for h in range(heads):
+        o_ref[:, h * HD : (h + 1) * HD] = result[h * rows : (h + 1) * rows]
+
+
+def attend(flags, queries, pairs, bias):
+    row_count, width = queries.shape
+    stacked_rows = BLOCK * (width // HD)
+    return pl.pallas_call(
+        attend_kernel,
+        out_shape=jax.ShapeDtypeStruct((row_count, width), jnp.bfloat16),
+        grid_spec=pltpu.PrefetchScalarGridSpec(
+            num_scalar_prefetch=1,
+            grid=(row_count // BLOCK,),
+            in_specs=[
+                pl.BlockSpec((BLOCK, width), lambda i, f: (i, 0)),
+                pl.BlockSpec(pairs.shape, lambda i, f: (0, 0)),
+                pl.BlockSpec((BLOCK, bias.shape[1]), lambda i, f: (i, 0)),
+            ],
+            out_specs=pl.BlockSpec((BLOCK, width), lambda i, f: (i, 0)),
+            scratch_shapes=[pltpu.VMEM((stacked_rows, HD), jnp.float32)] * 3,
+        ),
+        compiler_params=pltpu.CompilerParams(vmem_limit_bytes=40 * 2**20),
+        cost_estimate=pl.CostEstimate(
+            flops=4 * row_count * width * pairs.shape[0],
+            bytes_accessed=2 * pairs.size + 2 * bias.size + 4 * queries.size,
+            transcendentals=row_count * width // HD * pairs.shape[0],
+        ),
+    )(flags, queries, pairs, bias)
+
+
+def residual_kernel(places, att_ref, hidden_ref, gain_ref, *rest):
+    count = (len(rest) - 4) // 1
+    weights = rest[:count]
+    residual_ref, normed_ref, held, sems = rest[count:]
+    loads = [pltpu.make_async_copy(weights[m], held.at[m], sems.at[m]) for m in range(count)]
+    for load in loads:
+        load.start()
+    rows, depth = att_ref.shape[1], att_ref.shape[2]
+    width = hidden_ref.shape[2]
+    tile = 256
+    for m in range(count):
+        loads[m].wait()
+
+        def one(i, carry, m=m):
+            span = pl.ds(pl.multiple_of(i * tile, tile), tile)
+            terms = jnp.zeros((tile, width), jnp.float32)
+            for b in range(count):
+                terms += (
+                    jnp.dot(att_ref[b, span, :], held[m, b], preferred_element_type=jnp.float32)
+                    .astype(jnp.bfloat16)
+                    .astype(jnp.float32)
+                )
+            row_values = hidden_ref[places[m], span, :].astype(jnp.float32)
+            residual_ref[m, span, :] = (row_values + terms).astype(jnp.bfloat16)
+            return carry
+
+        lax.fori_loop(0, rows // tile, one, 0)
+
+    def norm(i, carry):
+        span = pl.ds(pl.multiple_of(i * 64, 64), 64)
+        squares = jnp.zeros((64, 1), jnp.float32)
+        for m in range(count):
+            widened = residual_ref[m, span, :].astype(jnp.float32)
+            squares += jnp.sum(widened * widened, axis=1, keepdims=True)
+        scale = lax.rsqrt(squares / (count * width) + epsilon)
+        for m in range(count):
+            widened = residual_ref[m, span, :].astype(jnp.float32)
+            normed_ref[m, span, :] = (widened * scale * gain_ref[m]).astype(jnp.bfloat16)
+        return carry
+
+    lax.fori_loop(0, rows // 64, norm, 0)
+
+
+def residual_and_norm(places, attended, hidden_pieces, gains, weights):
+    count = len(weights)
+    vmem = pl.BlockSpec(memory_space=pltpu.VMEM)
+    shape = jax.ShapeDtypeStruct(hidden_pieces.shape, jnp.bfloat16)
+    return pl.pallas_call(
+        residual_kernel,
+        out_shape=(shape, shape),
+        in_specs=[pl.BlockSpec(memory_space=pltpu.SMEM), vmem, vmem, vmem]
+        + [pl.BlockSpec(memory_space=pl.ANY)] * count,
+        out_specs=(vmem, vmem),
+        scratch_shapes=[
+            pltpu.VMEM((count,) + weights[0].shape, jnp.bfloat16),
+            pltpu.SemaphoreType.DMA((count,)),
+        ],
+        compiler_params=pltpu.CompilerParams(vmem_limit_bytes=48 * 2**20),
+        cost_estimate=pl.CostEstimate(
+            flops=2 * attended.size * hidden_pieces.shape[2] * count,
+            bytes_accessed=2 * count * weights[0].size + 6 * hidden_pieces.size,
+            transcendentals=0,
+        ),
+    )(places, attended, hidden_pieces, gains, *weights)
+
+
+def gate_up_kernel(x_ref, *rest):
+    out_ref = rest[-1]
+    count = x_ref.shape[0]
+    gate = jnp.zeros(out_ref.shape, jnp.float32)
+    up = jnp.zeros(out_ref.shape, jnp.float32)
+    for m in range(count):
+        gate += jnp.dot(x_ref[m], rest[m][...], preferred_element_type=jnp.float32)
+    for m in range(count):
+        up += jnp.dot(x_ref[m], rest[count + m][...], preferred_element_type=jnp.float32)
+    out_ref[...] = (gate / (1.0 + jnp.exp(-gate)) * up).astype(jnp.bfloat16)
+
+
+def gate_up(x, gates, ups):
+    count, rows, depth = x.shape
+    hidden_units = gates[0].shape[1]
+    tile = 256
+    return pl.pallas_call(
+        gate_up_kernel,
+        out_shape=jax.ShapeDtypeStruct((rows, hidden_units), jnp.bfloat16),
+        grid=(hidden_units // tile,),
+        in_specs=[pl.BlockSpec(x.shape, lambda i: (0, 0, 0))]
+        + [pl.BlockSpec((depth, tile), lambda i: (0, i))] * (2 * count),
+        out_specs=pl.BlockSpec((rows, tile), lambda i: (0, i)),
+        compiler_params=pltpu.CompilerParams(vmem_limit_bytes=48 * 2**20),
+        cost_estimate=pl.CostEstimate(
+            flops=4 * x.size * hidden_units,
+            bytes_accessed=4 * count * gates[0].size + 2 * x.size,
+            transcendentals=rows * hidden_units,
+        ),
+    )(x, *gates, *ups)
+
+
+def down_kernel(places, active_ref, *rest):
+    count = len(rest) - 3
+    weights = rest[:count]
+    out_ref, held, sems = rest[count:]
+    loads = [pltpu.make_async_copy(weights[m], held.at[m], sems.at[m]) for m in range(count)]
+    for load in loads:
+        load.start()
+    tile = 256
+    for m in range(count):
+        loads[m].wait()
+
+        def one(i, carry, m=m):
+            span = pl.ds(pl.multiple_of(i * tile, tile), tile)
+            out_ref[places[m], span, :] = lax.dot_general(
+                active_ref[span, :],
+                held[m],
+                (((1,), (1,)), ((), ())),
+                preferred_element_type=jnp.float32,
+            ).astype(jnp.bfloat16)
+            return carry
+
+        lax.fori_loop(0, active_ref.shape[0] // tile, one, 0)
+
+
+def down_terms_of(places, active, weights):
+    count = len(weights)
+    rows = active.shape[0]
+    width = weights[0].shape[0]
+    vmem = pl.BlockSpec(memory_space=pltpu.VMEM)
+    return pl.pallas_call(
+        down_kernel,
+        out_shape=jax.ShapeDtypeStruct((count, rows, width), jnp.bfloat16),
+        in_specs=[pl.BlockSpec(memory_space=pltpu.SMEM), vmem]
+        + [pl.BlockSpec(memory_space=pl.ANY)] * count,
+        out_specs=vmem,
+        scratch_shapes=[
+            pltpu.VMEM((count,) + weights[0].shape, jnp.bfloat16),
+            pltpu.SemaphoreType.DMA((count,)),
+        ],
+        compiler_params=pltpu.CompilerParams(vmem_limit_bytes=48 * 2**20),
+        cost_estimate=pl.CostEstimate(
+            flops=2 * active.size * width * count,
+            bytes_accessed=2 * count * weights[0].size + 2 * active.size,
+            transcendentals=0,
+        ),
+    )(places, active, *weights)
+
+
+def square_body(
+    hidden,
+    modality,
+    segment_bounds,
+    block_mask,
+    norm_gain,
+    query_weight,
+    keys_values,
+    output_weight,
+    gate_weight,
+    up_weight,
+    down_weight,
+):
+    seq_count = lax.axis_size("seq")
+    seq_index = lax.axis_index("seq")
+    tp_index = lax.axis_index("tp")
+    group = seq_count // 2
+    row_count, width = hidden.shape
+    weight_set = (seq_index >= group).astype(jnp.int32)
+    member = seq_index % group
+    places = member ^ jnp.arange(group, dtype=jnp.int32)
+    positions = seq_index * row_count + jnp.arange(row_count, dtype=jnp.int32)
+    segment_ids, offsets = segment_info(positions, segment_bounds)
+    gain_rows = lax.dynamic_index_in_dim(norm_gain, weight_set, 0, keepdims=False)
+    local_query = lax.dynamic_index_in_dim(query_weight, weight_set, 0, keepdims=False)
+    local_pairs = lax.dynamic_index_in_dim(keys_values, weight_set, 0, keepdims=False)
+
+    hidden_pieces = lax.all_gather(hidden, "tp", axis=0, tiled=False)
+    gate_far = exchange(gate_weight, 2)
+    up_far = exchange(up_weight, 2)
+    gate_near = exchange(gate_weight, 1)
+    up_near = exchange(up_weight, 1)
+    modes = lax.all_gather(modality, "seq", axis=0, tiled=True)
+
+    key_count = modes.shape[0]
+    key_positions = jnp.arange(key_count, dtype=jnp.int32)
+    key_segments = segment_info(key_positions, segment_bounds)[0]
+    block_rows = row_count // BLOCK
+    mask_rows = lax.dynamic_slice_in_dim(block_mask, seq_index * block_rows, block_rows, 0)
+    coarse = jnp.broadcast_to(
+        (mask_rows == 1)[:, None, :, None], (block_rows, BLOCK, key_count // BLOCK, BLOCK)
+    ).reshape(row_count, key_count)
+    mutual = (modality[:, None] > 0) & (modality[:, None] == modes[None, :])
+    allowed = (
+        coarse
+        & (segment_ids[:, None] == key_segments[None, :])
+        & ((key_positions[None, :] <= positions[:, None]) | mutual)
+    )
+    bias = jnp.where(allowed, 0.0, masked_score).astype(jnp.bfloat16)
+    flags = jnp.any(
+        allowed.reshape(block_rows, BLOCK, key_count // key_step, key_step), axis=(1, 3)
+    ).astype(jnp.int32)
+
+    full_rows = jnp.concatenate([hidden_pieces[c] for c in range(group)], axis=1)
+    normed = normalize(full_rows, gain_rows[0])
+    projected = jnp.dot(normed, local_pairs, preferred_element_type=jnp.float32).astype(
+        jnp.bfloat16
+    )
+    edge = (tp_index == 0) | (tp_index == 3)
+    left_part, right_part = projected[:, :HD], projected[:, HD:]
+    first = lax.ppermute(
+        jnp.where(edge, right_part, left_part), "tp", [(0, 1), (1, 2), (2, 0), (3, 3)]
+    )
+    second = lax.ppermute(
+        jnp.where(edge, left_part, right_part), "tp", [(0, 0), (1, 3), (2, 1), (3, 2)]
+    )
+    raw_keys = jnp.where(edge, second, first)
+    own_values = jnp.where(edge, first, second)
+    own_keys = rotary(raw_keys.astype(jnp.float32)[:, None, :], offsets)[:, 0, :].astype(
+        jnp.bfloat16
+    )
+    pairs = lax.all_gather(
+        jnp.concatenate([own_keys, own_values], axis=1), "seq", axis=0, tiled=True
+    )
+    queries = (
+        rotary(
+            jnp.dot(normed, local_query, preferred_element_type=jnp.float32).reshape(
+                row_count, -1, HD
+            ),
+            offsets,
+        )
+        .astype(jnp.bfloat16)
+        .reshape(row_count, -1)
+    )
+
+    output_slice = lax.dynamic_slice(
+        output_weight,
+        (weight_set, 0, member * width),
+        (1, output_weight.shape[1], width),
+    )[0]
+    output_slice, projected_tied = lax.optimization_barrier((output_slice, projected))
+    output_own = lax.all_gather(output_slice, "tp", axis=0, tiled=False)
+    output_far = exchange(output_own, 2)
+    output_near = exchange(output_own, 1)
+    output_diagonal = exchange(output_far, 1)
+    down_tied, output_own = lax.optimization_barrier((down_weight, output_own))
+    down_far = exchange(down_tied, 2)
+    down_near = exchange(down_tied, 1)
+
+    gate_far, up_far, pairs = lax.optimization_barrier((gate_far, up_far, pairs))
+    gate_diagonal = exchange(gate_far, 1)
+    up_diagonal = exchange(up_far, 1)
+
+    attended = attend(flags, queries, pairs, bias)
+    attended_all = lax.all_gather(attended, "tp", axis=0, tiled=False)
+    gains = gain_rows[1].reshape(group, 1, width)[places]
+    residual_pieces, normed_pieces = residual_and_norm(
+        places,
+        attended_all,
+        hidden_pieces,
+        gains,
+        (output_own, output_near, output_far, output_diagonal),
+    )
+    down_far, normed_pieces = lax.optimization_barrier((down_far, normed_pieces))
+    down_diagonal = exchange(down_far, 1)
+    active = gate_up(
+        normed_pieces,
+        (gate_weight, gate_near, gate_far, gate_diagonal),
+        (up_weight, up_near, up_far, up_diagonal),
+    )
+    terms = down_terms_of(places, active, (down_weight, down_near, down_far, down_diagonal))
+    down_share = lax.psum_scatter(terms, "tp", scatter_dimension=0, tiled=False)
+    residual_share = lax.dynamic_index_in_dim(
+        residual_pieces, member ^ tp_index, 0, keepdims=False
+    )
+    return (residual_share.astype(jnp.float32) + down_share.astype(jnp.float32)).astype(
+        jnp.bfloat16
+    )
+
+
 def solution(mesh):
     placed = (
         P("seq", "tp"),
@@ -237,6 +588,7 @@
         P("seq", "tp"),
         P("seq", "tp"),
     )
+    square = mesh.shape["seq"] == 2 * KVH and mesh.shape["tp"] == KVH
     return jax.shard_map(
-        body, mesh=mesh, in_specs=placed, out_specs=P("seq", "tp"), check_vma=False
-    )
+        square_body if square else general_body, mesh=mesh, in_specs=placed, out_specs=P("seq", "tp"), check_vma=False
+    )

time: 869 us -> 629 us (0.72)
  waiting for transfers between devices: 552 us -> 274 us
  blocking collectives: 7.79 us -> 198 us
  matrix products: 133 us -> 3.43 us
  other arithmetic: 117 us -> 19.4 us
  Pallas kernels: 0 us -> 76.9 us
  local copies, waits for them, and re-layouts: 40.4 us -> 28.5 us
  starting transfers between devices: 4.35 us -> 15.9 us
    ppermute x4 -> x14, waiting for transfers between devices: 270 us -> 0.04 us  [the longest x12 0.03 us: exchange(): lax.ppermute(block, 'seq', [(low, low ^ bit) for low in range(count)])]
    all_gather x1, blocking collectives: 7.79 us -> 198 us  [square_body(): modes = lax.all_gather(modality, 'seq', axis=0, tiled=True)]
    unnamed x9 -> x5, waiting for transfers between devices: 137 us -> 0.78 us
    dot_general x30 -> x2, matrix products: 133 us -> 3.43 us  [the longest x1 2.25 us: square_body(): jnp.dot(normed, local_query, preferred_element_type=jnp.float32)]
    select_n x12 -> x2, other arithmetic: 81.3 us -> 0.03 us  [the longest x1 0.02 us: square_body(): jnp.where(edge, left_part, right_part)]
    pallas_call x0 -> x4, Pallas kernels: none -> 76.9 us  [the longest x1 27.6 us: gate_up(): pl.pallas_call(gate_up_kernel, out_shape=jax.ShapeDtypeStruct((rows, hidd...]
    reduce_scatter x0 -> x1, waiting for transfers between devices: none -> 67.3 us  [square_body(): down_share = lax.psum_scatter(terms, 'tp', scatter_dimension=0, tiled=False)]
    all_gather x5 -> x4, waiting for transfers between devices: 144 us -> 206 us  [the longest x1 73.3 us: square_body(): hidden_pieces = lax.all_gather(hidden, 'tp', axis=0, tiled=False)]
  transfers between devices with their start and end apart: 11 -> 19, of which waited for: 7 -> 5; matrix products, arithmetic and copies ran while one was open for 30% -> 5% of each run, Pallas kernels for 0% -> 10%
where the time goes in v1:
time: 629 us
  waiting for transfers between devices  274 us (44%)
  blocking collectives  198 us (31%)
  Pallas kernels  76.9 us (12%)
  local copies, waits for them, and re-layouts  28.5 us (5%)
  other arithmetic  19.4 us (3%)
  starting transfers between devices  15.9 us (3%)
  between operations  13.5 us (2%)
    all_gather x1, blocking collectives, square_body(): modes = lax.all_gather(modality, 'seq', axis=0, tiled=True)  198 us
    all_gather x1, waiting for transfers between devices, square_body(): hidden_pieces = lax.all_gather(hidden, 'tp', axis=0, tiled=False)  73.3 us
    reduce_scatter x1, waiting for transfers between devices, square_body(): down_share = lax.psum_scatter(terms, 'tp', scatter_dimension=0, tiled=False)  67.3 us
    all_gather x1, waiting for transfers between devices, square_body(): output_own = lax.all_gather(output_slice, 'tp', axis=0, tiled=False)  64.5 us
    all_gather x1, waiting for transfers between devices, square_body(): attended_all = lax.all_gather(attended, 'tp', axis=0, tiled=False)  55.5 us
    pallas_call x1, Pallas kernels, gate_up(): pl.pallas_call(gate_up_kernel, out_shape=jax.ShapeDtypeStruct((rows, hidd...  27.6 us
    pallas_call x1, Pallas kernels, residual_and_norm(): pl.pallas_call(residual_kernel, out_shape=(shape, shape), in_specs=[pl.Bl...  18.3 us
    pallas_call x1, Pallas kernels, down_terms_of(): pl.pallas_call(down_kernel, out_shape=jax.ShapeDtypeStruct((count, rows,...  17 us
  transfers between devices with their start and end apart: 19, of which 5 were waited for; matrix products, arithmetic and copies ran while one was open for 5% of the time, Pallas kernels for 10%

profile of v1, /device:TPU:0, one launch (start us, length us, event | category | flops | bytes accessed | tf_op | source)
XLA Modules:
  0.0 629.5 jit_solution(7015411737865025395)
XLA Ops:
  6.5 0.7 all-gather.11.cloned.1.call-update
  7.3 0.9 dynamic-slice_reduce_fusion
  8.2 2.2 dynamic-slice_bitcast_fusion.1
  10.4 73.3 %all-gather.11.cloned.1.call-done = bf16[2048,896]{1,0:T(8,128)(2,1)} async-done(((bf16[512,896]{1,0:T(8,128)(2,1)}), bf16[2048,896]{1,0:T(8,128)(2,1)}) %all-gather.11.cloned.1.call-update) | async-done | bytes 3670032 | tf_op jit(solution)/shard_map/all_gather | solution.py:474
  83.8 2.5 fusion.28
  86.2 0.9 fusion.2
  87.2 1.2 fusion.10
  88.5 1.6 collective-permute-start
  90.0 0.5 collective-permute-start.1
  90.7 4.1 dynamic-slice_bitcast_fusion
  94.8 64.5 %all-gather.15.cloned.1.call-done = bf16[2048,896]{1,0:T(8,128)(2,1)} async-done(((bf16[512,896]{1,0:T(8,128)(2,1)}), bf16[2048,896]{1,0:T(8,128)(2,1)}) %all-gather.15.cloned.1.call-update) | async-done | bytes 3670032 | tf_op jit(solution)/shard_map/all_gather | solution.py:538
  159.3 1.5 collective-permute-start.5
  160.8 0.7 collective-permute-start.2
  161.5 4.6 collective-permute-start.3
  166.1 0.7 dynamic-slice_compare_fusion
  166.8 6.0 copy.19
  172.9 197.6 %all-gather.3 = s32[8,1,512]{2,1,0:T(1,128)S(1)} all-gather(s32[1,1,512]{2,1,0:T(1,128)S(1)} %bitcast.54), channel_id=1, replica_groups=mesh['seq'=8,'tp'=4] {'seq'}, dimensions={0}, use_global_device_ids=true | all-gather | bytes 18432 | tf_op jit(solution)/shard_map/all_gather | solution.py:479
  370.6 0.4 collective-permute-start.10
  371.0 1.2 fusion.21
  372.4 0.8 pad_maximum_fusion.2
  373.2 0.2 all-gather.13.cloned.1.call-start
  373.5 4.7 and_reduce_fusion
  378.5 0.5 multiply_cosine_fusion.1
  379.1 0.6 broadcast_in_dim.23
  379.7 7.0 %select_convert_fusion.bias_ref = bf16[512,4096]{1,0:T(8,128)(2,1)} fusion(pred[64,8,32,128]{3,2,1,0:T(8,128)(4,1)S(1)} %bitcast.46, s32[4096]{0:T(1024)S(1)} %bitcast.51, s32[512]{0:T(512)S(1)} %iota_add_fusion, s32[4096]{0:T(1024)S(1)} %convert_reduce_fusion, s32[512]{0:T(512)S(1)} %copy-done.7, s32[512]{0:T(512)S(1)} %get-tuple-element.28, ...), kind=kLoop, calls=%fused_computation.3 | loop fusion | flops 18874368 | bytes 6330880 | tf_op jit(solution)/shard_map/convert_element_type | solution.py:495
  386.9 0.3 collective-permute-start.6
  387.2 2.3 fusion.5
  389.5 1.5 collective-permute-start.7
  391.2 0.2 copy.22.q_ref
  391.5 12.8 %all-gather.9.cloned.1.call-done.kv_ref = bf16[4096,256]{1,0:T(8,128)(2,1)} async-done(((bf16[512,256]{1,0:T(8,128)(2,1)}), bf16[4096,256]{1,0:T(8,128)(2,1)}) %all-gather.9.cloned.1.call-update) | async-done | bytes 2097168 | tf_op jit(solution)/shard_map/all_gather | solution.py:518
  404.3 2.2 copy-done
  406.5 1.6 copy-done.2
  408.1 13.9 %shard_map.109 = bf16[512,512]{1,0:T(8,128)(2,1)} custom-call(s32[4,8]{1,0:T(4,128)S(1)} %convert_element_type.58.flags, bf16[512,512]{1,0:T(8,128)(2,1)S(1)} %copy.22.q_ref, bf16[4096,256]{1,0:T(8,128)(2,1)S(1)} %copy-done.2, bf16[512,4096]{1,0:T(8,128)(2,1)S(1)} %copy-done), custom_call_target="tpu_custom_call" | custom-call | flops 4294967296 | bytes 7340032 | tf_op jit(solution)/shard_map/pallas_call | solution.py:278
  422.0 0.3 reduce-scatter.2.cloned.1.call-start
  422.3 3.0 collective-permute-start.8
  425.4 0.4 collective-permute-start.9
  425.8 0.6 gather_fusion
  426.4 55.5 %all-gather.13.cloned.1.call-done = bf16[2048,512]{1,0:T(8,128)(2,1)} async-done(((bf16[512,512]{1,0:T(8,128)(2,1)}), bf16[2048,512]{1,0:T(8,128)(2,1)}) %all-gather.13.cloned.1.call-update) | async-done | bytes 2097168 | tf_op jit(solution)/shard_map/all_gather | solution.py:551
  481.9 1.6 copy-done.3
  483.5 18.3 %shard_map.110 = (bf16[4,512,896]{2,1,0:T(8,128)(2,1)S(1)}, bf16[4,512,896]{2,1,0:T(8,128)(2,1)}) custom-call(s32[4]{0:T(128)S(1)} %iota_xor_fusion.places, bf16[4,512,512]{2,1,0:T(8,128)(2,1)S(1)} %bitcast.45, bf16[4,512,896]{2,1,0:T(8,128)(2,1)} %bitcast.47, f32[4,1,896]{2,1,0:T(1,128)S(1)} %reshape.220.gain_ref, bf16[4,512,896]{2,1,0:T(8,128)(2,1)} %bitcast.21.rest_0_, ...), custom_call_target="tpu_custom_call" | custom-call | flops 7516192768 | bytes 25690112 | tf_op jit(solution)/shard_map/pallas_call | solution.py:348
  501.9 1.8 copy-done.1
  503.6 0.5 collective-permute-start.13
  504.2 27.6 %shard_map.111.active_ref = bf16[512,2560]{1,0:T(8,128)(2,1)S(1)} custom-call(bf16[4,512,896]{2,1,0:T(8,128)(2,1)} %get-tuple-element.21.x_ref, bf16[896,2560]{1,0:T(8,128)(2,1)} %rest_0_.2, bf16[896,2560]{1,0:T(8,128)(2,1)} %collective-permute-done.8.rest_1_, bf16[896,2560]{1,0:T(8,128)(2,1)} %collective-permute-done.rest_2_, ...), custom_call_target="tpu_custom_call" | custom-call | flops 18790481920 | bytes 40370176 | tf_op jit(solution)/shard_map/pallas_call | solution.py:383
  531.8 2.1 copy-done.9
  533.9 2.1 copy-done.10
  536.0 17.0 %shard_map.112 = bf16[4,512,896]{2,1,0:T(8,128)(2,1)} custom-call(s32[4]{0:T(128)S(1)} %iota_xor_fusion.places, bf16[512,2560]{1,0:T(8,128)(2,1)S(1)} %shard_map.111.active_ref, bf16[896,2560]{1,0:T(8,128)(2,1)} %rest_0_.3, bf16[896,2560]{1,0:T(8,128)(2,1)} %copy-done.9, bf16[896,2560]{1,0:T(8,128)(2,1)} %collective-permute-done.7.rest_2_, ...), custom_call_target="tpu_custom_call" | custom-call | flops 9395240960 | bytes 20971520 | tf_op jit(solution)/shard_map/pallas_call | solution.py:428
  553.1 67.3 %reduce-scatter.2.cloned.1.call-done = bf16[1,512,896]{2,1,0:T(8,128)(2,1)} async-done(((bf16[4,512,896]{2,1,0:T(8,128)(2,1)}), bf16[1,512,896]{2,1,0:T(8,128)(2,1)}) %reduce-scatter.2.cloned.1.call-update) | async-done | bytes 917520 | tf_op jit(solution)/shard_map/reduce_scatter | solution.py:568
  620.4 2.6 fusion.15
  (69 shorter events, 1.6 us)
Async XLA Ops:
  6.5 77.2 %all-gather.11.cloned.1.call-start = ((), (), s32[]{:S(2)}) async-start(), calls=%async_computation.3 | async-start | bytes 4587520 | tf_op jit(solution)/shard_map/all_gather | solution.py:474
  7.3 152.0 %all-gather.15.cloned.1.call-start = ((), (), s32[]{:S(2)}) async-start(), calls=%async_computation.5 | async-start | bytes 4587520 | tf_op jit(solution)/shard_map/all_gather | solution.py:538
  83.8 3.4 copy-start.11
  86.2 1.0 copy-start.5
  87.2 3.4 copy-start.8
  88.4 315.9 %all-gather.9.cloned.1.call-start = ((), (), s32[]{:S(2)}) async-start(), calls=%async_computation.1 | async-start | bytes 2359296 | tf_op jit(solution)/shard_map/all_gather | solution.py:518
  88.5 301.0 %collective-permute-start = (bf16[896,2560]{1,0:T(8,128)(2,1)}, bf16[896,2560]{1,0:T(8,128)(2,1)}, u32[]{:S(2)}, u32[]{:S(2)}) collective-permute-start(bf16[896,2560]{1,0:T(8,128)(2,1)} %rest_0_.2), channel_id=1, source_target_pairs={{0,8},{4,12},{8,0},{12,4},{16,24},{20,28},{24,16},{28,20},{1,9},{5... | collective-permute-start | bytes 13762568 | tf_op jit(solution)/shard_map/ppermute | solution.py:230
  90.0 301.4 %collective-permute-start.1 = (bf16[896,2560]{1,0:T(8,128)(2,1)}, bf16[896,2560]{1,0:T(8,128)(2,1)}, u32[]{:S(2)}, u32[]{:S(2)}) collective-permute-start(bf16[896,2560]{1,0:T(8,128)(2,1)} %rest_4_.1), channel_id=1, source_target_pairs={{0,8},{4,12},{8,0},{12,4},{16,24},{20,28},{24,16},{28,20},{1,9},{5... | collective-permute-start | bytes 13762568 | tf_op jit(solution)/shard_map/ppermute | solution.py:230
  94.8 78.1 %copy-start.7 = (s32[512]{0:T(512)S(1)}, s32[512]{0:T(512)}, u32[]{:S(2)}) copy-start(s32[512]{0:T(512)} %param.12) | copy-start | bytes 6148
  159.3 227.6 %collective-permute-start.5 = (bf16[4,512,896]{2,1,0:T(8,128)(2,1)}, bf16[4,512,896]{2,1,0:T(8,128)(2,1)}, u32[]{:S(2)}, u32[]{:S(2)}) collective-permute-start(bf16[4,512,896]{2,1,0:T(8,128)(2,1)} %bitcast.21.rest_0_), channel_id=1, source_target_pairs={{0,8},{4,12},{8,0},{12,4},{16,24},{20,28},{24,16},{28,20},{1,9},{5... | collective-permute-start | bytes 11010056 | tf_op jit(solution)/shard_map/ppermute | solution.py:230
  160.8 209.8 %collective-permute-start.2 = (bf16[512,128]{1,0:T(8,128)(2,1)S(1)}, bf16[512,128]{1,0:T(8,128)(2,1)S(1)}, u32[]{:S(2)}, u32[]{:S(2)}) collective-permute-start(bf16[512,128]{1,0:T(8,128)(2,1)S(1)} %get-tuple-element.39), channel_id=1, source_target_pairs={{0,0},{1,3},{2,1},{3,2},{4,4},{5,7},{6,5},{7,6},{8,8},{9,11},{10,9... | collective-permute-start | bytes 393224 | tf_op jit(solution)/shard_map/ppermute | solution.py:510
  161.5 209.5 %collective-permute-start.3 = (bf16[512,128]{1,0:T(8,128)(2,1)S(1)}, bf16[512,128]{1,0:T(8,128)(2,1)S(1)}, u32[]{:S(2)}, u32[]{:S(2)}) collective-permute-start(bf16[512,128]{1,0:T(8,128)(2,1)S(1)} %get-tuple-element.40), channel_id=1, source_target_pairs={{0,1},{1,2},{2,0},{3,3},{4,5},{5,6},{6,4},{7,7},{8,9},{9,10},{10,8... | collective-permute-start | bytes 393224 | tf_op jit(solution)/shard_map/ppermute | solution.py:507
  370.6 133.0 %collective-permute-start.10 = (bf16[896,2560]{1,0:T(8,128)(2,1)}, bf16[896,2560]{1,0:T(8,128)(2,1)}, u32[]{:S(2)}, u32[]{:S(2)}) collective-permute-start(bf16[896,2560]{1,0:T(8,128)(2,1)} %rest_4_.1), channel_id=1, source_target_pairs={{0,4},{4,0},{8,12},{12,8},{16,20},{20,16},{24,28},{28,24},{1,5},{5... | collective-permute-start | bytes 13762568 | tf_op jit(solution)/shard_map/ppermute | solution.py:230
  373.2 108.7 %all-gather.13.cloned.1.call-start = ((), (), s32[]{:S(2)}) async-start(), calls=%async_computation.4 | async-start | bytes 2621440 | tf_op jit(solution)/shard_map/all_gather | solution.py:551
  379.1 8.1 %copy-start.4 = (bf16[512,3584]{1,0:T(8,128)(2,1)S(1)}, bf16[512,3584]{1,0:T(8,128)(2,1)}, u32[]{:S(2)}) copy-start(bf16[512,3584]{1,0:T(8,128)(2,1)} %copy.19) | copy-start | bytes 11010052
  379.1 8.1 %copy-start.6 = (bf16[512,896]{1,0:T(8,128)(2,1)S(1)}, bf16[512,896]{1,0:T(8,128)(2,1)}, u32[]{:S(2)}) copy-start(bf16[512,896]{1,0:T(8,128)(2,1)} %copy-done.5) | copy-start | bytes 2752516
  386.7 38.6 %collective-permute-start.4 = (bf16[4,512,896]{2,1,0:T(8,128)(2,1)}, bf16[4,512,896]{2,1,0:T(8,128)(2,1)}, u32[]{:S(2)}, u32[]{:S(2)}) collective-permute-start(bf16[4,512,896]{2,1,0:T(8,128)(2,1)} %bitcast.21.rest_0_), channel_id=1, source_target_pairs={{0,4},{4,0},{8,12},{12,8},{16,20},{20,16},{24,28},{28,24},{1,5},{5... | collective-permute-start | bytes 11010056 | tf_op jit(solution)/shard_map/ppermute | solution.py:230
  386.9 38.5 %collective-permute-start.6 = (bf16[4,512,896]{2,1,0:T(8,128)(2,1)}, bf16[4,512,896]{2,1,0:T(8,128)(2,1)}, u32[]{:S(2)}, u32[]{:S(2)}) collective-permute-start(bf16[4,512,896]{2,1,0:T(8,128)(2,1)} %collective-permute-done.5.rest_2_), channel_id=1, source_target_pairs={{0,4},{4,0},{8,12},{12,8},{16,20},{20,16},{24,28},{28,24},{1,5},{5... | collective-permute-start | bytes 11010056 | tf_op jit(solution)/shard_map/ppermute | solution.py:230
  389.5 114.2 %collective-permute-start.7 = (bf16[896,2560]{1,0:T(8,128)(2,1)}, bf16[896,2560]{1,0:T(8,128)(2,1)}, u32[]{:S(2)}, u32[]{:S(2)}) collective-permute-start(bf16[896,2560]{1,0:T(8,128)(2,1)} %rest_0_.3), channel_id=1, source_target_pairs={{0,8},{4,12},{8,0},{12,4},{16,24},{20,28},{24,16},{28,20},{1,9},{5... | collective-permute-start | bytes 13762568 | tf_op jit(solution)/shard_map/ppermute | solution.py:230
  404.3 2.2 copy-start
  406.5 1.6 copy-start.2
  422.0 198.3 %reduce-scatter.2.cloned.1.call-start = ((), (), s32[]{:S(2)}) async-start(), calls=%async_computation.2 | async-start | bytes 4587520 | tf_op jit(solution)/shard_map/reduce_scatter | solution.py:568
  422.3 81.9 %collective-permute-start.8 = (bf16[896,2560]{1,0:T(8,128)(2,1)}, bf16[896,2560]{1,0:T(8,128)(2,1)}, u32[]{:S(2)}, u32[]{:S(2)}) collective-permute-start(bf16[896,2560]{1,0:T(8,128)(2,1)} %rest_0_.2), channel_id=1, source_target_pairs={{0,4},{4,0},{8,12},{12,8},{16,20},{20,16},{24,28},{28,24},{1,5},{5... | collective-permute-start | bytes 13762568 | tf_op jit(solution)/shard_map/ppermute | solution.py:230
  425.3 78.9 %collective-permute-start.11 = (bf16[896,2560]{1,0:T(8,128)(2,1)}, bf16[896,2560]{1,0:T(8,128)(2,1)}, u32[]{:S(2)}, u32[]{:S(2)}) collective-permute-start(bf16[896,2560]{1,0:T(8,128)(2,1)} %collective-permute-done.1.rest_6_), channel_id=1, source_target_pairs={{0,4},{4,0},{8,12},{12,8},{16,20},{20,16},{24,28},{28,24},{1,5},{5... | collective-permute-start | bytes 13762568 | tf_op jit(solution)/shard_map/ppermute | solution.py:230
  425.4 78.8 %collective-permute-start.9 = (bf16[896,2560]{1,0:T(8,128)(2,1)}, bf16[896,2560]{1,0:T(8,128)(2,1)}, u32[]{:S(2)}, u32[]{:S(2)}) collective-permute-start(bf16[896,2560]{1,0:T(8,128)(2,1)} %collective-permute-done.rest_2_), channel_id=1, source_target_pairs={{0,4},{4,0},{8,12},{12,8},{16,20},{20,16},{24,28},{28,24},{1,5},{5... | collective-permute-start | bytes 13762568 | tf_op jit(solution)/shard_map/ppermute | solution.py:230
  481.9 1.6 copy-start.3
  501.8 1.8 copy-start.1
  503.6 28.2 %collective-permute-start.12 = (bf16[896,2560]{1,0:T(8,128)(2,1)}, bf16[896,2560]{1,0:T(8,128)(2,1)S(1)}, u32[]{:S(2)}, u32[]{:S(2)}) collective-permute-start(bf16[896,2560]{1,0:T(8,128)(2,1)} %rest_0_.3), channel_id=1, source_target_pairs={{0,4},{4,0},{8,12},{12,8},{16,20},{20,16},{24,28},{28,24},{1,5},{5... | collective-permute-start | bytes 13762568 | tf_op jit(solution)/shard_map/ppermute | solution.py:230
  503.6 28.2 %collective-permute-start.13 = (bf16[896,2560]{1,0:T(8,128)(2,1)}, bf16[896,2560]{1,0:T(8,128)(2,1)S(1)}, u32[]{:S(2)}, u32[]{:S(2)}) collective-permute-start(bf16[896,2560]{1,0:T(8,128)(2,1)} %collective-permute-done.7.rest_2_), channel_id=1, source_target_pairs={{0,4},{4,0},{8,12},{12,8},{16,20},{20,16},{24,28},{28,24},{1,5},{5... | collective-permute-start | bytes 13762568 | tf_op jit(solution)/shard_map/ppermute | solution.py:230
  531.8 2.1 copy-start.9
  533.9 2.1 copy-start.10
Sparse Core Ops, SparseCore 0:
  8.9 74.7 all-gather.10
  88.5 70.7 all-gather.14
  373.3 30.9 all-gather.8
  422.1 59.7 all-gather.12
  553.2 67.0 reduce-scatter.1

commit v2 on v1

--- a/solution.py
+++ b/solution.py
@@ -1,3 +1,5 @@
+import functools
+
 import jax
 import jax.numpy as jnp
 from jax import lax
@@ -298,114 +300,106 @@
     )(flags, queries, pairs, bias)
 
 
-def residual_kernel(places, att_ref, hidden_ref, gain_ref, *rest):
-    count = (len(rest) - 4) // 1
-    weights = rest[:count]
-    residual_ref, normed_ref, held, sems = rest[count:]
-    loads = [pltpu.make_async_copy(weights[m], held.at[m], sems.at[m]) for m in range(count)]
-    for load in loads:
-        load.start()
-    rows, depth = att_ref.shape[1], att_ref.shape[2]
-    width = hidden_ref.shape[2]
-    tile = 256
-    for m in range(count):
-        loads[m].wait()
-
-        def one(i, carry, m=m):
-            span = pl.ds(pl.multiple_of(i * tile, tile), tile)
-            terms = jnp.zeros((tile, width), jnp.float32)
-            for b in range(count):
-                terms += (
-                    jnp.dot(att_ref[b, span, :], held[m, b], preferred_element_type=jnp.float32)
-                    .astype(jnp.bfloat16)
-                    .astype(jnp.float32)
+def output_kernel(chosen, att_ref, weight_ref, out_ref):
+    out_ref[0] = jnp.dot(
+        att_ref[...], weight_ref[0], preferred_element_type=jnp.float32
+    ).astype(jnp.bfloat16)
+
+
+def output_terms(chosen, attended, output_weight, width):
+    rows, depth = attended.shape
+    count = output_weight.shape[2] // width
+    return pl.pallas_call(
+        output_kernel,
+        out_shape=jax.ShapeDtypeStruct((count, rows, width), jnp.bfloat16),
+        grid_spec=pltpu.PrefetchScalarGridSpec(
+            num_scalar_prefetch=1,
+            grid=(count,),
+            in_specs=[
+                pl.BlockSpec((rows, depth), lambda c, f: (0, 0)),
+                pl.BlockSpec((1, depth, width), lambda c, f: (f[0], 0, c)),
+            ],
+            out_specs=pl.BlockSpec((1, rows, width), lambda c, f: (c, 0, 0)),
+        ),
+        compiler_params=pltpu.CompilerParams(vmem_limit_bytes=32 * 2**20),
+        cost_estimate=pl.CostEstimate(
+            flops=2 * attended.size * width * count,
+            bytes_accessed=2 * depth * width * count + 2 * rows * width * count,
+            transcendentals=0,
+        ),
+    )(chosen, attended, output_weight)
+
+
+def gate_up_kernel(counts, places, x_ref, *rest):
+    out_ref = rest[-1]
+    at = 0
+    totals = []
+    for layout in counts:
+        total = jnp.zeros(out_ref.shape, jnp.float32)
+        for m, parts in enumerate(layout):
+            first = 0
+            for depth in parts:
+                total += jnp.dot(
+                    x_ref[places[m], :, first : first + depth],
+                    rest[at][...],
+                    preferred_element_type=jnp.float32,
                 )
-            row_values = hidden_ref[places[m], span, :].astype(jnp.float32)
-            residual_ref[m, span, :] = (row_values + terms).astype(jnp.bfloat16)
-            return carry
-
-        lax.fori_loop(0, rows // tile, one, 0)
-
-    def norm(i, carry):
-        span = pl.ds(pl.multiple_of(i * 64, 64), 64)
-        squares = jnp.zeros((64, 1), jnp.float32)
-        for m in range(count):
-            widened = residual_ref[m, span, :].astype(jnp.float32)
-            squares += jnp.sum(widened * widened, axis=1, keepdims=True)
-        scale = lax.rsqrt(squares / (count * width) + epsilon)
-        for m in range(count):
-            widened = residual_ref[m, span, :].astype(jnp.float32)
-            normed_ref[m, span, :] = (widened * scale * gain_ref[m]).astype(jnp.bfloat16)
-        return carry
-
-    lax.fori_loop(0, rows // 64, norm, 0)
-
-
-def residual_and_norm(places, attended, hidden_pieces, gains, weights):
-    count = len(weights)
-    vmem = pl.BlockSpec(memory_space=pltpu.VMEM)
-    shape = jax.ShapeDtypeStruct(hidden_pieces.shape, jnp.bfloat16)
-    return pl.pallas_call(
-        residual_kernel,
-        out_shape=(shape, shape),
-        in_specs=[pl.BlockSpec(memory_space=pltpu.SMEM), vmem, vmem, vmem]
-        + [pl.BlockSpec(memory_space=pl.ANY)] * count,
-        out_specs=(vmem, vmem),
-        scratch_shapes=[
-            pltpu.VMEM((count,) + weights[0].shape, jnp.bfloat16),
-            pltpu.SemaphoreType.DMA((count,)),
-        ],
-        compiler_params=pltpu.CompilerParams(vmem_limit_bytes=48 * 2**20),
-        cost_estimate=pl.CostEstimate(
-            flops=2 * attended.size * hidden_pieces.shape[2] * count,
-            bytes_accessed=2 * count * weights[0].size + 6 * hidden_pieces.size,
-            transcendentals=0,
-        ),
-    )(places, attended, hidden_pieces, gains, *weights)
-
-
-def gate_up_kernel(x_ref, *rest):
-    out_ref = rest[-1]
-    count = x_ref.shape[0]
-    gate = jnp.zeros(out_ref.shape, jnp.float32)
-    up = jnp.zeros(out_ref.shape, jnp.float32)
-    for m in range(count):
-        gate += jnp.dot(x_ref[m], rest[m][...], preferred_element_type=jnp.float32)
-    for m in range(count):
-        up += jnp.dot(x_ref[m], rest[count + m][...], preferred_element_type=jnp.float32)
+                first += depth
+                at += 1
+        totals.append(total)
+    gate, up = totals
     out_ref[...] = (gate / (1.0 + jnp.exp(-gate)) * up).astype(jnp.bfloat16)
 
 
-def gate_up(x, gates, ups):
+def gate_up(places, x, gates, ups):
     count, rows, depth = x.shape
-    hidden_units = gates[0].shape[1]
+    arrays = [part for piece in gates + ups for part in piece]
+    counts = [[[part.shape[0] for part in piece] for piece in pieces] for pieces in (gates, ups)]
+    hidden_units = arrays[0].shape[1]
     tile = 256
     return pl.pallas_call(
-        gate_up_kernel,
+        functools.partial(gate_up_kernel, counts),
         out_shape=jax.ShapeDtypeStruct((rows, hidden_units), jnp.bfloat16),
-        grid=(hidden_units // tile,),
-        in_specs=[pl.BlockSpec(x.shape, lambda i: (0, 0, 0))]
-        + [pl.BlockSpec((depth, tile), lambda i: (0, i))] * (2 * count),
-        out_specs=pl.BlockSpec((rows, tile), lambda i: (0, i)),
+        grid_spec=pltpu.PrefetchScalarGridSpec(
+            num_scalar_prefetch=1,
+            grid=(hidden_units // tile,),
+            in_specs=[pl.BlockSpec(x.shape, lambda i, f: (0, 0, 0))]
+            + [pl.BlockSpec((part.shape[0], tile), lambda i, f: (0, i)) for part in arrays],
+            out_specs=pl.BlockSpec((rows, tile), lambda i, f: (0, i)),
+        ),
         compiler_params=pltpu.CompilerParams(vmem_limit_bytes=48 * 2**20),
         cost_estimate=pl.CostEstimate(
             flops=4 * x.size * hidden_units,
-            bytes_accessed=4 * count * gates[0].size + 2 * x.size,
+            bytes_accessed=4 * count * depth * hidden_units + 2 * x.size,
             transcendentals=rows * hidden_units,
         ),
-    )(x, *gates, *ups)
-
-
-def down_kernel(places, active_ref, *rest):
-    count = len(rest) - 3
-    weights = rest[:count]
-    out_ref, held, sems = rest[count:]
-    loads = [pltpu.make_async_copy(weights[m], held.at[m], sems.at[m]) for m in range(count)]
+    )(places, x, *arrays)
+
+
+def down_kernel(counts, places, active_ref, *rest):
+    total = sum(len(parts) for parts in counts)
+    weights = rest[:total]
+    out_ref, held, sems = rest[total:]
+    loads = []
+    at = 0
+    for m, parts in enumerate(counts):
+        first = 0
+        for depth in parts:
+            loads.append(
+                pltpu.make_async_copy(
+                    weights[at], held.at[m, first : first + depth], sems.at[at]
+                )
+            )
+            first += depth
+            at += 1
     for load in loads:
         load.start()
     tile = 256
-    for m in range(count):
-        loads[m].wait()
+    at = 0
+    for m, parts in enumerate(counts):
+        for _ in parts:
+            loads[at].wait()
+            at += 1
 
         def one(i, carry, m=m):
             span = pl.ds(pl.multiple_of(i * tile, tile), tile)
@@ -420,28 +414,30 @@
         lax.fori_loop(0, active_ref.shape[0] // tile, one, 0)
 
 
-def down_terms_of(places, active, weights):
-    count = len(weights)
-    rows = active.shape[0]
-    width = weights[0].shape[0]
+def down_terms_of(places, active, pieces):
+    count = len(pieces)
+    rows, hidden_units = active.shape
+    arrays = [part for piece in pieces for part in piece]
+    counts = [[part.shape[0] for part in piece] for piece in pieces]
+    width = sum(counts[0])
     vmem = pl.BlockSpec(memory_space=pltpu.VMEM)
     return pl.pallas_call(
-        down_kernel,
+        functools.partial(down_kernel, counts),
         out_shape=jax.ShapeDtypeStruct((count, rows, width), jnp.bfloat16),
         in_specs=[pl.BlockSpec(memory_space=pltpu.SMEM), vmem]
-        + [pl.BlockSpec(memory_space=pl.ANY)] * count,
+        + [pl.BlockSpec(memory_space=pl.ANY)] * len(arrays),
         out_specs=vmem,
         scratch_shapes=[
-            pltpu.VMEM((count,) + weights[0].shape, jnp.bfloat16),
-            pltpu.SemaphoreType.DMA((count,)),
+            pltpu.VMEM((count, width, hidden_units), jnp.bfloat16),
+            pltpu.SemaphoreType.DMA((len(arrays),)),
         ],
         compiler_params=pltpu.CompilerParams(vmem_limit_bytes=48 * 2**20),
         cost_estimate=pl.CostEstimate(
             flops=2 * active.size * width * count,
-            bytes_accessed=2 * count * weights[0].size + 2 * active.size,
+            bytes_accessed=2 * count * width * hidden_units + 2 * active.size,
             transcendentals=0,
         ),
-    )(places, active, *weights)
+    )(places, active, *arrays)
 
 
 def square_body(
@@ -471,12 +467,17 @@
     local_query = lax.dynamic_index_in_dim(query_weight, weight_set, 0, keepdims=False)
     local_pairs = lax.dynamic_index_in_dim(keys_values, weight_set, 0, keepdims=False)
 
+    modes = lax.all_gather(modality, "seq", axis=0, tiled=True)
+    gate_tied, modes = lax.optimization_barrier((gate_weight, modes))
     hidden_pieces = lax.all_gather(hidden, "tp", axis=0, tiled=False)
-    gate_far = exchange(gate_weight, 2)
-    up_far = exchange(up_weight, 2)
+    depth = gate_weight.shape[0]
+    long_cut = depth * 5 // 7 // 128 * 128
+    short_cut = depth - long_cut
+    gate_far_a = exchange(gate_tied[:long_cut], 2)
+    gate_far_b = exchange(gate_tied[long_cut:], 2)
+    hidden_pieces, gate_far_a = lax.optimization_barrier((hidden_pieces, gate_far_a))
     gate_near = exchange(gate_weight, 1)
     up_near = exchange(up_weight, 1)
-    modes = lax.all_gather(modality, "seq", axis=0, tiled=True)
 
     key_count = modes.shape[0]
     key_positions = jnp.arange(key_count, dtype=jnp.int32)
@@ -515,9 +516,16 @@
     own_keys = rotary(raw_keys.astype(jnp.float32)[:, None, :], offsets)[:, 0, :].astype(
         jnp.bfloat16
     )
-    pairs = lax.all_gather(
-        jnp.concatenate([own_keys, own_values], axis=1), "seq", axis=0, tiled=True
-    )
+    own_pairs = jnp.concatenate([own_keys, own_values], axis=1)
+    own_pairs, gate_far_b = lax.optimization_barrier((own_pairs, gate_far_b))
+    pairs = lax.all_gather(own_pairs, "seq", axis=0, tiled=True)
+    pairs, up_tied, down_tied, gate_far_a, gate_far_b = lax.optimization_barrier(
+        (pairs, up_weight, down_weight, gate_far_a, gate_far_b)
+    )
+    up_far_a = exchange(up_tied[:short_cut], 2)
+    up_far_b = exchange(up_tied[short_cut:], 2)
+    gate_diagonal_a = exchange(gate_far_a, 1)
+    gate_diagonal_b = exchange(gate_far_b, 1)
     queries = (
         rotary(
             jnp.dot(normed, local_query, preferred_element_type=jnp.float32).reshape(
@@ -529,46 +537,40 @@
         .reshape(row_count, -1)
     )
 
-    output_slice = lax.dynamic_slice(
-        output_weight,
-        (weight_set, 0, member * width),
-        (1, output_weight.shape[1], width),
-    )[0]
-    output_slice, projected_tied = lax.optimization_barrier((output_slice, projected))
-    output_own = lax.all_gather(output_slice, "tp", axis=0, tiled=False)
-    output_far = exchange(output_own, 2)
-    output_near = exchange(output_own, 1)
-    output_diagonal = exchange(output_far, 1)
-    down_tied, output_own = lax.optimization_barrier((down_weight, output_own))
-    down_far = exchange(down_tied, 2)
+    attended = attend(flags, queries, pairs, bias)
+    attended, up_far_a, down_tied = lax.optimization_barrier((attended, up_far_a, down_tied))
+    up_diagonal_a = exchange(up_far_a, 1)
     down_near = exchange(down_tied, 1)
-
-    gate_far, up_far, pairs = lax.optimization_barrier((gate_far, up_far, pairs))
-    gate_diagonal = exchange(gate_far, 1)
-    up_diagonal = exchange(up_far, 1)
-
-    attended = attend(flags, queries, pairs, bias)
-    attended_all = lax.all_gather(attended, "tp", axis=0, tiled=False)
-    gains = gain_rows[1].reshape(group, 1, width)[places]
-    residual_pieces, normed_pieces = residual_and_norm(
+    half = depth // 2
+    down_far_a = exchange(down_tied[:half], 2)
+    down_far_b = exchange(down_tied[half:], 2)
+    attention_terms = output_terms(weight_set[None], attended, output_weight, width)
+    attention_share = lax.psum_scatter(attention_terms, "tp", scatter_dimension=0, tiled=False)
+    attention_share, up_far_b = lax.optimization_barrier((attention_share, up_far_b))
+    up_diagonal_b = exchange(up_far_b, 1)
+    residual_share = (hidden.astype(jnp.float32) + attention_share.astype(jnp.float32)).astype(
+        jnp.bfloat16
+    )
+    residual_pieces = lax.all_gather(residual_share, "tp", axis=0, tiled=False)
+    residual_pieces, down_far_a = lax.optimization_barrier((residual_pieces, down_far_a))
+    down_diagonal_a = exchange(down_far_a, 1)
+    widened = residual_pieces.astype(jnp.float32)
+    mean_square = jnp.mean(widened * widened, axis=(0, 2), keepdims=True)
+    gains = gain_rows[1].reshape(group, 1, width)
+    second_normed = (widened * lax.rsqrt(mean_square + epsilon) * gains).astype(jnp.bfloat16)
+    active = gate_up(
         places,
-        attended_all,
-        hidden_pieces,
-        gains,
-        (output_own, output_near, output_far, output_diagonal),
-    )
-    down_far, normed_pieces = lax.optimization_barrier((down_far, normed_pieces))
-    down_diagonal = exchange(down_far, 1)
-    active = gate_up(
-        normed_pieces,
-        (gate_weight, gate_near, gate_far, gate_diagonal),
-        (up_weight, up_near, up_far, up_diagonal),
-    )
-    terms = down_terms_of(places, active, (down_weight, down_near, down_far, down_diagonal))
+        second_normed,
+        [[gate_weight], [gate_near], [gate_far_a, gate_far_b], [gate_diagonal_a, gate_diagonal_b]],
+        [[up_weight], [up_near], [up_far_a, up_far_b], [up_diagonal_a, up_diagonal_b]],
+    )
+    down_diagonal_b = exchange(down_far_b, 1)
+    terms = down_terms_of(
+        places,
+        active,
+        [[down_weight], [down_near], [down_far_a, down_far_b], [down_diagonal_a, down_diagonal_b]],
+    )
     down_share = lax.psum_scatter(terms, "tp", scatter_dimension=0, tiled=False)
-    residual_share = lax.dynamic_index_in_dim(
-        residual_pieces, member ^ tp_index, 0, keepdims=False
-    )
     return (residual_share.astype(jnp.float32) + down_share.astype(jnp.float32)).astype(
         jnp.bfloat16
     )

time: 629 us -> 507 us (0.81)
  blocking collectives: 198 us -> 10.5 us
  waiting for transfers between devices: 274 us -> 326 us
  local copies, waits for them, and re-layouts: 28.5 us -> 43.5 us
  Pallas kernels: 76.9 us -> 66 us
  other arithmetic: 19.4 us -> 28.1 us
    ppermute x12 -> x15, waiting for transfers between devices: 0.03 us -> 221 us  [exchange(): lax.ppermute(block, 'seq', [(low, low ^ bit) for low in range(count)])]
    all_gather x1, blocking collectives: 198 us -> 10.5 us  [square_body(): modes = lax.all_gather(modality, 'seq', axis=0, tiled=True)]
    all_gather x3 -> x2, waiting for transfers between devices: 133 us -> 25.1 us  [the longest x1 21.6 us: square_body(): residual_pieces = lax.all_gather(residual_share, 'tp', axis=0, tiled=False)]
    all_gather x1, waiting for transfers between devices: 73.3 us -> 0.01 us  [square_body(): hidden_pieces = lax.all_gather(hidden, 'tp', axis=0, tiled=False)]
    pallas_call x3, Pallas kernels: 63 us -> 50.1 us  [the longest x1 28.6 us: gate_up(): pl.pallas_call(functools.partial(gate_up_kernel, counts), out_shape=jax.S...]
    slice x2 -> x6, local copies, waits for them, and re-layouts: 3.36 us -> 15.6 us  [the longest x1 4.16 us: square_body(): gate_far_a = exchange(gate_tied[:long_cut], 2)]
    reduce_scatter x1, waiting for transfers between devices: 67.3 us -> 76 us  [square_body(): down_share = lax.psum_scatter(terms, 'tp', scatter_dimension=0, tiled=False)]
  transfers between devices with their start and end apart: 19 -> 22, of which waited for: 5 -> 11; matrix products, arithmetic and copies ran while one was open for 5% -> 12% of each run, Pallas kernels for 10% -> 9%
where the time goes in v2:
time: 507 us; the launch traced here: 510 us
  waiting for transfers between devices  326 us (64%)
  Pallas kernels  66 us (13%)
  local copies, waits for them, and re-layouts  43.5 us (9%)
  other arithmetic  28.1 us (6%)
  starting transfers between devices  17.3 us (3%)
  between operations  13.5 us (3%)
  blocking collectives  10.5 us (2%)
  matrix products  5.65 us (1%)
    ppermute x15, waiting for transfers between devices, exchange(): lax.ppermute(block, 'seq', [(low, low ^ bit) for low in range(count)])  221 us
    reduce_scatter x1, waiting for transfers between devices, square_body(): down_share = lax.psum_scatter(terms, 'tp', scatter_dimension=0, tiled=False)  76 us
    pallas_call x1, Pallas kernels, gate_up(): pl.pallas_call(functools.partial(gate_up_kernel, counts), out_shape=jax.S...  28.6 us
    all_gather x1, waiting for transfers between devices, square_body(): residual_pieces = lax.all_gather(residual_share, 'tp', axis=0, tiled=False)  21.6 us
    pallas_call x1, Pallas kernels, down_terms_of(): pl.pallas_call(functools.partial(down_kernel, counts), out_shape=jax.Shap...  18.3 us
    pallas_call x1, Pallas kernels, attend(): pl.pallas_call(attend_kernel, out_shape=jax.ShapeDtypeStruct((row_count,...  15.9 us
    unnamed x46, local copies, waits for them, and re-layouts  12.4 us
    all_gather x1, blocking collectives, square_body(): modes = lax.all_gather(modality, 'seq', axis=0, tiled=True)  10.5 us
  transfers between devices with their start and end apart: 22, of which 11 were waited for; matrix products, arithmetic and copies ran while one was open for 12% of the time, Pallas kernels for 9%

profile of v2, /device:TPU:0, one launch (start us, length us, event | category | flops | bytes accessed | tf_op | source)
XLA Modules:
  0.0 510.2 jit_solution(6654901248044287697)
XLA Ops:
  7.3 10.5 %all-gather.2 = s32[8,1,512]{2,1,0:T(1,128)S(1)} all-gather(s32[1,1,512]{2,1,0:T(1,128)} %bitcast.64), channel_id=1, replica_groups=mesh['seq'=8,'tp'=4] {'seq'}, dimensions={0}, use_global_device_ids=true | all-gather | bytes 18432 | tf_op jit(solution)/shard_map/all_gather | solution.py:470
  17.8 4.2 slice.61
  22.0 1.3 collective-permute-start
  23.3 2.5 slice.73
  26.7 69.3 %collective-permute-done.rest_2_ = bf16[640,2560]{1,0:T(8,128)(2,1)} collective-permute-done((bf16[640,2560]{1,0:T(8,128)(2,1)}, bf16[640,2560]{1,0:T(8,128)(2,1)}, u32[]{:S(2)}, u32[]{:S(2)}) %collective-permute-start) | collective-permute-done | bytes 3276832 | tf_op jit(solution)/shard_map/ppermute | solution.py:232
  96.0 2.3 slice_bitcast_fusion.3
  98.3 0.9 fusion.2
  99.3 1.8 copy-done.18
  101.0 1.2 fusion.14
  102.9 7.3 %collective-permute-start.2 = (bf16[512,128]{1,0:T(8,128)(2,1)S(1)}, bf16[512,128]{1,0:T(8,128)(2,1)S(1)}, u32[]{:S(2)}, u32[]{:S(2)}) collective-permute-start(bf16[512,128]{1,0:T(8,128)(2,1)S(1)} %get-tuple-element.58), channel_id=1, source_target_pairs={{0,1},{1,2},{2,0},{3,3},{4,5},{5,6},{6,4},{7,7},{8,9},{9,10},{10,8... | collective-permute-start | bytes 393224 | tf_op jit(solution)/shard_map/ppermute | solution.py:508
  110.3 2.6 collective-permute-done.2
  112.9 1.2 fusion.24
  115.0 8.4 %collective-permute-done.3.rest_3_ = bf16[256,2560]{1,0:T(8,128)(2,1)S(1)} collective-permute-done((bf16[256,2560]{1,0:T(8,128)(2,1)}, bf16[256,2560]{1,0:T(8,128)(2,1)S(1)}, u32[]{:S(2)}, u32[]{:S(2)}) %collective-permute-start.3) | collective-permute-done | bytes 1310752 | tf_op jit(solution)/shard_map/ppermute | solution.py:232
  123.7 4.3 dynamic-slice_bitcast_fusion
  127.9 6.0 %copy.19 = bf16[512,3584]{1,0:T(8,128)(2,1)} copy(bf16[512,3584]{0,1:T(8,128)(2,1)} %dynamic-slice_bitcast_fusion) | data formatting | bytes 7340032 | tf_op jit(solution)/shard_map/dot_general | solution.py:531
  134.9 4.8 and_reduce_fusion
  141.2 7.0 %select_convert_fusion.bias_ref = bf16[512,4096]{1,0:T(8,128)(2,1)} fusion(pred[64,8,32,128]{3,2,1,0:T(8,128)(4,1)S(1)} %bitcast.55, s32[4096]{0:T(1024)S(1)} %bitcast.61, s32[512]{0:T(512)S(1)} %iota_add_fusion, s32[4096]{0:T(1024)S(1)} %convert_reduce_fusion, s32[512]{0:T(512)S(1)} %copy-done.15, s32[512]{0:T(512)S(1)} %get-tuple-element.44, ...), kind=kLoop, calls=%fused_computation.4 | loop fusion | flops 18874368 | bytes 6330880 | tf_op jit(solution)/shard_map/convert_element_type | solution.py:496
  148.1 3.6 all-gather.7.cloned.1.call-done.kv_ref
  151.7 2.5 slice.74
  154.2 1.5 collective-permute-start.4
  155.7 4.5 fusion.8
  161.2 2.2 copy.22.q_ref
  163.4 2.2 copy-done.1
  165.6 1.0 copy-done.2
  166.6 1.6 copy-done.3
  168.2 15.9 %shard_map.109.att_ref = bf16[512,512]{1,0:T(8,128)(2,1)S(1)} custom-call(s32[4,8]{1,0:T(4,128)S(1)} %convert_element_type.73.flags, bf16[512,512]{1,0:T(8,128)(2,1)S(1)} %copy-done.2, bf16[4096,256]{1,0:T(8,128)(2,1)S(1)} %copy-done.3, bf16[512,4096]{1,0:T(8,128)(2,1)S(1)} %copy-done.1), custom_call_target="tpu_custom_call" | custom-call | flops 4294967296 | bytes 7340032 | tf_op jit(solution)/shard_map/pallas_call | solution.py:280
  184.1 1.3 collective-permute-done.4.rest_8_
  185.5 3.2 shard_map.110
  188.7 1.9 copy-done
  190.7 2.2 slice.75
  192.9 1.5 collective-permute-start.5
  194.9 70.4 %collective-permute-done.5.rest_9_ = bf16[640,2560]{1,0:T(8,128)(2,1)} collective-permute-done((bf16[640,2560]{1,0:T(8,128)(2,1)S(1)}, bf16[640,2560]{1,0:T(8,128)(2,1)}, u32[]{:S(2)}, u32[]{:S(2)}) %collective-permute-start.5) | collective-permute-done | bytes 3276832 | tf_op jit(solution)/shard_map/ppermute | solution.py:232
  265.3 2.3 add_convert_fusion
  267.9 4.1 fusion.30
  272.0 1.5 collective-permute-start.6
  274.7 3.7 collective-permute-done.9.rest_5_
  278.4 1.1 copy-done.7
  279.6 45.2 %collective-permute-done.6.rest_2_ = bf16[448,2560]{1,0:T(8,128)(2,1)S(1)} collective-permute-done((bf16[448,2560]{1,0:T(8,128)(2,1)S(1)}, bf16[448,2560]{1,0:T(8,128)(2,1)S(1)}, u32[]{:S(2)}, u32[]{:S(2)}) %collective-permute-start.6) | collective-permute-done | bytes 2293792 | tf_op jit(solution)/shard_map/ppermute | solution.py:232
  324.8 21.6 %all-gather.11.cloned.1.call-done = bf16[2048,896]{1,0:T(8,128)(2,1)} async-done(((bf16[512,896]{1,0:T(8,128)(2,1)}), bf16[2048,896]{1,0:T(8,128)(2,1)}) %all-gather.11.cloned.1.call-update) | async-done | bytes 3670032 | tf_op jit(solution)/shard_map/all_gather | solution.py:554
  346.4 3.0 fusion.5
  349.4 22.8 %collective-permute-done.14.rest_3_ = bf16[448,2560]{1,0:T(8,128)(2,1)} collective-permute-done((bf16[448,2560]{1,0:T(8,128)(2,1)}, bf16[448,2560]{1,0:T(8,128)(2,1)}, u32[]{:S(2)}, u32[]{:S(2)}) %collective-permute-start.14) | collective-permute-done | bytes 2293792 | tf_op jit(solution)/shard_map/ppermute | solution.py:232
  372.7 2.9 fusion.7.x_ref
  375.6 28.6 %shard_map.111.active_ref = bf16[512,2560]{1,0:T(8,128)(2,1)} custom-call(s32[4]{0:T(128)S(1)} %iota_xor_fusion.places, bf16[4,512,896]{2,1,0:T(8,128)(2,1)} %fusion.7.x_ref, bf16[896,2560]{1,0:T(8,128)(2,1)} %rest_0_.2, bf16[896,2560]{1,0:T(8,128)(2,1)} %collective-permute-done.7.rest_1_, bf16[640,2560]{1,0:T(8,128)(2,1)} %collective-permute-done.rest_2_, ...), custom_call_target="tpu_custom_call" | custom-call | flops 18790481920 | bytes 40370176 | tf_op jit(solution)/shard_map/pallas_call | solution.py:360
  404.2 1.4 copy-done.19
  405.6 1.4 copy-done.20
  407.0 18.3 %shard_map.112 = bf16[4,512,896]{2,1,0:T(8,128)(2,1)} custom-call(s32[4]{0:T(128)S(1)} %iota_xor_fusion.places, bf16[512,2560]{1,0:T(8,128)(2,1)} %shard_map.111.active_ref, bf16[896,2560]{1,0:T(8,128)(2,1)} %rest_0_.3, bf16[896,2560]{1,0:T(8,128)(2,1)} %collective-permute-done.13.rest_1_, bf16[448,2560]{1,0:T(8,128)(2,1)S(1)} %collective-permute-done.6.rest_2_, ...), custom_call_target="tpu_custom_call" | custom-call | flops 9395240960 | bytes 20971520 | tf_op jit(solution)/shard_map/pallas_call | solution.py:424
  425.3 76.0 %reduce-scatter.5.cloned.1.call-done = bf16[1,512,896]{2,1,0:T(8,128)(2,1)} async-done(((bf16[4,512,896]{2,1,0:T(8,128)(2,1)}), bf16[1,512,896]{2,1,0:T(8,128)(2,1)}) %reduce-scatter.5.cloned.1.call-update) | async-done | bytes 917520 | tf_op jit(solution)/shard_map/reduce_scatter | solution.py:573
  501.3 2.3 fusion.10
  (102 shorter events, 9.7 us)
Async XLA Ops:
  6.5 89.5 %all-gather.9.cloned.1.call-start = ((), (), s32[]{:S(2)}) async-start(), calls=%async_computation.5 | async-start | bytes 4587520 | tf_op jit(solution)/shard_map/all_gather | solution.py:472
  7.3 144.4 %all-gather.7.cloned.1.call-start = ((), (), s32[]{:S(2)}) async-start(), calls=%async_computation.2 | async-start | bytes 2359296 | tf_op jit(solution)/shard_map/all_gather | solution.py:521
  17.8 8.7 %copy-start.16 = (f32[2,2,3584]{2,1,0:T(2,128)S(1)}, f32[2,2,3584]{2,1,0:T(2,128)}, u32[]{:S(2)}) copy-start(f32[2,2,3584]{2,1,0:T(2,128)} %param.15) | copy-start | bytes 172036
  17.8 8.8 %copy-start.17 = (s32[6]{0:T(128)S(1)}, s32[6]{0:T(128)}, u32[]{:S(2)}) copy-start(s32[6]{0:T(128)} %param.13) | copy-start | bytes 76
  22.0 74.0 %collective-permute-start = (bf16[640,2560]{1,0:T(8,128)(2,1)}, bf16[640,2560]{1,0:T(8,128)(2,1)}, u32[]{:S(2)}, u32[]{:S(2)}) collective-permute-start(bf16[640,2560]{1,0:T(8,128)(2,1)} %slice.61), channel_id=1, source_target_pairs={{0,8},{4,12},{8,0},{12,4},{16,24},{20,28},{24,16},{28,20},{1,9},{5... | collective-permute-start | bytes 9830408 | tf_op jit(solution)/shard_map/ppermute | solution.py:232
  25.8 97.6 %collective-permute-start.3 = (bf16[256,2560]{1,0:T(8,128)(2,1)}, bf16[256,2560]{1,0:T(8,128)(2,1)S(1)}, u32[]{:S(2)}, u32[]{:S(2)}) collective-permute-start(bf16[256,2560]{1,0:T(8,128)(2,1)} %slice.73), channel_id=1, source_target_pairs={{0,8},{4,12},{8,0},{12,4},{16,24},{20,28},{24,16},{28,20},{1,9},{5... | collective-permute-start | bytes 3932168 | tf_op jit(solution)/shard_map/ppermute | solution.py:232
  98.3 3.9 copy-start.11
  98.3 3.9 copy-start.13
  98.3 2.7 copy-start.18
  102.3 8.0 %collective-permute-start.1 = (bf16[512,128]{1,0:T(8,128)(2,1)S(1)}, bf16[512,128]{1,0:T(8,128)(2,1)S(1)}, u32[]{:S(2)}, u32[]{:S(2)}) collective-permute-start(bf16[512,128]{1,0:T(8,128)(2,1)S(1)} %get-tuple-element.57), channel_id=1, source_target_pairs={{0,0},{1,3},{2,1},{3,2},{4,4},{5,7},{6,5},{7,6},{8,8},{9,11},{10,9... | collective-permute-start | bytes 393224 | tf_op jit(solution)/shard_map/ppermute | solution.py:511
  102.9 9.9 %collective-permute-start.2 = (bf16[512,128]{1,0:T(8,128)(2,1)S(1)}, bf16[512,128]{1,0:T(8,128)(2,1)S(1)}, u32[]{:S(2)}, u32[]{:S(2)}) collective-permute-start(bf16[512,128]{1,0:T(8,128)(2,1)S(1)} %get-tuple-element.58), channel_id=1, source_target_pairs={{0,1},{1,2},{2,0},{3,3},{4,5},{5,6},{6,4},{7,7},{8,9},{9,10},{10,8... | collective-permute-start | bytes 393224 | tf_op jit(solution)/shard_map/ppermute | solution.py:508
  123.4 4.5 copy-start.4
  123.4 141.9 %reduce-scatter.3.cloned.1.call-start = ((), (), s32[]{:S(2)}) async-start(), calls=%async_computation.3 | async-start | bytes 4587520 | tf_op jit(solution)/shard_map/reduce_scatter | solution.py:548
  127.9 6.9 %copy-start.15 = (s32[512]{0:T(512)S(1)}, s32[512]{0:T(512)}, u32[]{:S(2)}) copy-start(s32[512]{0:T(512)} %param.12) | copy-start | bytes 6148
  141.2 14.5 %copy-start.12 = (bf16[512,896]{1,0:T(8,128)(2,1)S(1)}, bf16[512,896]{1,0:T(8,128)(2,1)}, u32[]{:S(2)}) copy-start(bf16[512,896]{1,0:T(8,128)(2,1)} %copy-done.11) | copy-start | bytes 2752516
  154.2 31.3 %collective-permute-start.4 = (bf16[256,2560]{1,0:T(8,128)(2,1)}, bf16[256,2560]{1,0:T(8,128)(2,1)}, u32[]{:S(2)}, u32[]{:S(2)}) collective-permute-start(bf16[256,2560]{1,0:T(8,128)(2,1)} %slice.74), channel_id=1, source_target_pairs={{0,8},{4,12},{8,0},{12,4},{16,24},{20,28},{24,16},{28,20},{1,9},{5... | collective-permute-start | bytes 3932168 | tf_op jit(solution)/shard_map/ppermute | solution.py:232
  161.2 24.3 %slice-start = ((s8[7340032]{0:T(1024)(128)(4,1)}), s8[3145728]{0:T(1024)(128)(4,1)S(1)}, s32[]{:S(2)}) async-start(s8[7340032]{0:T(1024)(128)(4,1)} %bitcast.51), calls=%async_computation.7 | async-start | bytes 6291456
  163.4 2.2 copy-start.1
  165.6 1.0 copy-start.2
  166.6 1.6 copy-start.3
  168.2 17.3 %slice-start.1 = ((s8[7340032]{0:T(1024)(128)(4,1)}), s8[4194304]{0:T(1024)(128)(4,1)S(1)}, s32[]{:S(2)}) async-start(s8[7340032]{0:T(1024)(128)(4,1)} %bitcast.51), calls=%async_computation.8 | async-start | bytes 8388608
  188.7 1.9 copy-start
  190.6 74.7 %copy-start.14 = (bf16[512,896]{1,0:T(8,128)(2,1)S(1)}, bf16[512,896]{1,0:T(8,128)(2,1)}, u32[]{:S(2)}) copy-start(bf16[512,896]{1,0:T(8,128)(2,1)} %param.11) | copy-start | bytes 2752516
  190.6 155.8 %all-gather.11.cloned.1.call-start = ((), (), s32[]{:S(2)}) async-start(), calls=%async_computation.6 | async-start | bytes 4587520 | tf_op jit(solution)/shard_map/all_gather | solution.py:554
  192.9 72.4 %collective-permute-start.5 = (bf16[640,2560]{1,0:T(8,128)(2,1)S(1)}, bf16[640,2560]{1,0:T(8,128)(2,1)}, u32[]{:S(2)}, u32[]{:S(2)}) collective-permute-start(bf16[640,2560]{1,0:T(8,128)(2,1)S(1)} %slice.75), channel_id=1, source_target_pairs={{0,8},{4,12},{8,0},{12,4},{16,24},{20,28},{24,16},{28,20},{1,9},{5... | collective-permute-start | bytes 9830408 | tf_op jit(solution)/shard_map/ppermute | solution.py:232
  194.4 79.6 %collective-permute-start.10 = (bf16[896,2560]{1,0:T(8,128)(2,1)}, bf16[896,2560]{1,0:T(8,128)(2,1)}, u32[]{:S(2)}, u32[]{:S(2)}) collective-permute-start(bf16[896,2560]{1,0:T(8,128)(2,1)} %rest_6_.1), channel_id=1, source_target_pairs={{0,4},{4,0},{8,12},{12,8},{16,20},{20,16},{24,28},{28,24},{1,5},{5... | collective-permute-start | bytes 13762568 | tf_op jit(solution)/shard_map/ppermute | solution.py:232
  194.4 79.6 %collective-permute-start.7 = (bf16[896,2560]{1,0:T(8,128)(2,1)}, bf16[896,2560]{1,0:T(8,128)(2,1)}, u32[]{:S(2)}, u32[]{:S(2)}) collective-permute-start(bf16[896,2560]{1,0:T(8,128)(2,1)} %rest_0_.2), channel_id=1, source_target_pairs={{0,4},{4,0},{8,12},{12,8},{16,20},{20,16},{24,28},{28,24},{1,5},{5... | collective-permute-start | bytes 13762568 | tf_op jit(solution)/shard_map/ppermute | solution.py:232
  267.7 233.7 %reduce-scatter.5.cloned.1.call-start = ((), (), s32[]{:S(2)}) async-start(), calls=%async_computation.4 | async-start | bytes 4587520 | tf_op jit(solution)/shard_map/reduce_scatter | solution.py:573
  267.9 5.6 %copy-start.5 = (bf16[256,2560]{1,0:T(8,128)(2,1)S(1)}, bf16[256,2560]{1,0:T(8,128)(2,1)}, u32[]{:S(2)}) copy-start(bf16[256,2560]{1,0:T(8,128)(2,1)} %copy-done.4) | copy-start | bytes 3932164
  272.0 52.8 %collective-permute-start.6 = (bf16[448,2560]{1,0:T(8,128)(2,1)S(1)}, bf16[448,2560]{1,0:T(8,128)(2,1)S(1)}, u32[]{:S(2)}, u32[]{:S(2)}) collective-permute-start(bf16[448,2560]{1,0:T(8,128)(2,1)S(1)} %get-tuple-element.46), channel_id=1, source_target_pairs={{0,8},{4,12},{8,0},{12,4},{16,24},{20,28},{24,16},{28,20},{1,9},{5... | collective-permute-start | bytes 6881288 | tf_op jit(solution)/shard_map/ppermute | solution.py:232
  273.5 4.9 collective-permute-start.9
  273.5 102.1 %collective-permute-start.8 = (bf16[640,2560]{1,0:T(8,128)(2,1)}, bf16[640,2560]{1,0:T(8,128)(2,1)}, u32[]{:S(2)}, u32[]{:S(2)}) collective-permute-start(bf16[640,2560]{1,0:T(8,128)(2,1)} %collective-permute-done.rest_2_), channel_id=1, source_target_pairs={{0,4},{4,0},{8,12},{12,8},{16,20},{20,16},{24,28},{28,24},{1,5},{5... | collective-permute-start | bytes 9830408 | tf_op jit(solution)/shard_map/ppermute | solution.py:232
  274.0 101.6 %collective-permute-start.12 = (bf16[640,2560]{1,0:T(8,128)(2,1)}, bf16[640,2560]{1,0:T(8,128)(2,1)}, u32[]{:S(2)}, u32[]{:S(2)}) collective-permute-start(bf16[640,2560]{1,0:T(8,128)(2,1)} %collective-permute-done.5.rest_9_), channel_id=1, source_target_pairs={{0,4},{4,0},{8,12},{12,8},{16,20},{20,16},{24,28},{28,24},{1,5},{5... | collective-permute-start | bytes 9830408 | tf_op jit(solution)/shard_map/ppermute | solution.py:232
  274.0 98.1 %collective-permute-start.14 = (bf16[448,2560]{1,0:T(8,128)(2,1)}, bf16[448,2560]{1,0:T(8,128)(2,1)}, u32[]{:S(2)}, u32[]{:S(2)}) collective-permute-start(bf16[448,2560]{1,0:T(8,128)(2,1)} %get-tuple-element.45), channel_id=1, source_target_pairs={{0,8},{4,12},{8,0},{12,4},{16,24},{20,28},{24,16},{28,20},{1,9},{5... | collective-permute-start | bytes 6881288 | tf_op jit(solution)/shard_map/ppermute | solution.py:232
  278.4 1.1 copy-start.7
  279.4 124.8 %collective-permute-start.13 = (bf16[896,2560]{1,0:T(8,128)(2,1)}, bf16[896,2560]{1,0:T(8,128)(2,1)}, u32[]{:S(2)}, u32[]{:S(2)}) collective-permute-start(bf16[896,2560]{1,0:T(8,128)(2,1)} %rest_0_.3), channel_id=1, source_target_pairs={{0,4},{4,0},{8,12},{12,8},{16,20},{20,16},{24,28},{28,24},{1,5},{5... | collective-permute-start | bytes 13762568 | tf_op jit(solution)/shard_map/ppermute | solution.py:232
  324.8 47.3 %collective-permute-start.11 = (bf16[256,2560]{1,0:T(8,128)(2,1)}, bf16[256,2560]{1,0:T(8,128)(2,1)}, u32[]{:S(2)}, u32[]{:S(2)}) collective-permute-start(bf16[256,2560]{1,0:T(8,128)(2,1)} %collective-permute-done.4.rest_8_), channel_id=1, source_target_pairs={{0,4},{4,0},{8,12},{12,8},{16,20},{20,16},{24,28},{28,24},{1,5},{5... | collective-permute-start | bytes 3932168 | tf_op jit(solution)/shard_map/ppermute | solution.py:232
  346.4 26.3 %copy-start.9 = (bf16[2048,896]{1,0:T(8,128)(2,1)S(1)}, bf16[2048,896]{1,0:T(8,128)(2,1)}, u32[]{:S(2)}) copy-start(bf16[2048,896]{1,0:T(8,128)(2,1)} %all-gather.11.cloned.1.call-done) | copy-start | bytes 11010052
  372.2 32.0 %collective-permute-start.16 = (bf16[448,2560]{1,0:T(8,128)(2,1)}, bf16[448,2560]{1,0:T(8,128)(2,1)S(1)}, u32[]{:S(2)}, u32[]{:S(2)}) collective-permute-start(bf16[448,2560]{1,0:T(8,128)(2,1)} %collective-permute-done.14.rest_3_), channel_id=1, source_target_pairs={{0,4},{4,0},{8,12},{12,8},{16,20},{20,16},{24,28},{28,24},{1,5},{5... | collective-permute-start | bytes 6881288 | tf_op jit(solution)/shard_map/ppermute | solution.py:232
  372.2 32.1 %collective-permute-start.15 = (bf16[448,2560]{1,0:T(8,128)(2,1)S(1)}, bf16[448,2560]{1,0:T(8,128)(2,1)S(1)}, u32[]{:S(2)}, u32[]{:S(2)}) collective-permute-start(bf16[448,2560]{1,0:T(8,128)(2,1)S(1)} %collective-permute-done.6.rest_2_), channel_id=1, source_target_pairs={{0,4},{4,0},{8,12},{12,8},{16,20},{20,16},{24,28},{28,24},{1,5},{5... | collective-permute-start | bytes 6881288 | tf_op jit(solution)/shard_map/ppermute | solution.py:232
  372.7 2.9 copy-start.6
  372.7 2.9 copy-start.8
  404.2 1.4 copy-start.19
  405.6 1.4 copy-start.20
  425.3 76.0 %copy-start.10 = (bf16[512,896]{1,0:T(8,128)(2,1)S(1)}, bf16[512,896]{1,0:T(8,128)(2,1)}, u32[]{:S(2)}) copy-start(bf16[512,896]{1,0:T(8,128)(2,1)} %add_convert_fusion) | copy-start | bytes 2752516
Sparse Core Ops, SparseCore 0:
  8.9 74.7 all-gather.8
  123.6 28.0 all-gather.6
  190.7 73.9 reduce-scatter.2
  267.8 78.5 all-gather.10
  425.5 75.8 reduce-scatter.4
